TPU v7x, 32 devices: a whole 2x2x4 slice. The times are simulated.
32 devices in a mesh: groups: 2 (over x), inst: 4 (over y, core), tp: 4 (over z).
Axes of the slice: x: 2, y: 2, z: 4, core: 2. Of those that a mesh axis runs over, the one named last changes fastest.
Arguments:
- x_new: bfloat16 [2, 384, 16384], P(None, ('groups', 'inst'), 'tp'), parts along dimension 1, may hold values from -6 to 6
- z_new: bfloat16 [2, 384, 16384], P(None, ('groups', 'inst'), 'tp'), parts along dimension 1, may hold values from -6 to 6
- ssm_state: bfloat16 [384, 16, 16384], P(('groups', 'inst'), None, 'tp'), parts along dimension 0, may hold values from -4 to 4
- conv_state: bfloat16 [384, 3, 16384], P(('groups', 'inst'), None, 'tp'), parts along dimension 0, may hold values from -6 to 6
- conv_weight: float32 [4, 16384], P(None, 'tp'), may hold values from -3 to 3
- conv_bias: float32 [16384], P('tp'), may hold values from -0.5 to 0.5
- proj_weight: bfloat16 [16384, 544], P('tp'), may hold values from -1.5 to 1.5
- dt_weight: bfloat16 [512, 16384], P(None, 'tp'), may hold values from -0.25 to 0.25
- dt_bias: float32 [16384], P('tp'), may hold values from -6 to -1
- a_log: float32 [16, 16384], P(None, 'tp'), may hold values from 0 to 2.77
- skip_gain: float32 [16384], P('tp'), may hold values from 0.5 to 2
- leave_slot: int32 [8, 12], P(('groups', 'inst')), parts along dimension 0, may hold values from 0 to 47, as said below
- dest_table: int32 [8, 12], P('groups'), parts along dimension 0, may hold values from 0 to 3, as said below
- land_slot: int32 [8, 12], P(('groups', 'inst')), parts along dimension 0, may hold values from 0 to 47, as said below
Outputs:
- outputs: bfloat16 [2, 384, 16384], P(None, ('groups', 'inst'), 'tp'), parts along dimension 1
- new_ssm: bfloat16 [384, 16, 16384], P(('groups', 'inst'), None, 'tp'), parts along dimension 0
- new_conv: bfloat16 [384, 3, 16384], P(('groups', 'inst'), None, 'tp'), parts along dimension 0
There are 2 independent parts, one for each index of `groups`. A program takes and returns all parts, laid end to end along the dimension named above; an argument that names none is the same for every part. Nothing has to cross between parts.
Inputs may be any that keep to these rules, and one draw needn't show every extreme that they name: `leave_slot`: each row holds 12 distinct slots. dest_table[i, k] is never i; every instance receives exactly 12 requests; no instance sends more than 4 to one destination, and every instance sends exactly 4 to some destination. `land_slot`: row j is a reordering of row j of leave_slot.
All inputs are finite; a program needn't handle non-finite values.
Results may differ from a plain program's by a relative error of at most 0.0056.
Values may be sent and summed in bfloat16 or wider, within the bound.
No kernel may reach another device: no remote copies, remote signals or barrier semaphores. Data moves between devices by JAX's collectives and lax.ppermute only.
A program may use at most 128 MiB of HBM per device.

v0:
```python
import jax
import jax.numpy as jnp
from jax import lax
from jax.sharding import PartitionSpec as P


def convolve(window, conv_weight, conv_bias):
    conv_sum = jnp.einsum("rjc,jc->rc", window.astype(jnp.float32), conv_weight) + conv_bias
    return jax.nn.silu(conv_sum)


def local(
    x_new,
    z_new,
    ssm_state,
    conv_state,
    conv_weight,
    conv_bias,
    proj_weight,
    dt_weight,
    dt_bias,
    a_log,
    skip_gain,
    leave_slot,
    dest_table,
    land_slot,
):
    slot_count = ssm_state.shape[0]
    migrate = leave_slot.shape[1]
    inst_count = lax.axis_size("inst")
    own_index = lax.axis_index("inst")
    flat_dest = dest_table.reshape(-1)
    arriving = flat_dest == own_index
    arrival_rank = jnp.cumsum(arriving.astype(jnp.int32)) - 1
    landing = jnp.take(land_slot[0], jnp.clip(arrival_rank, 0, migrate - 1))
    target_all = jnp.where(arriving, landing, slot_count)
    leaving = leave_slot[0]
    send_ssm = jnp.take(ssm_state, leaving, axis=0)
    send_conv = jnp.take(conv_state, leaving, axis=0)
    capacity = max(2, (migrate + inst_count - 2) // (inst_count - 1))
    own_dest = lax.dynamic_index_in_dim(dest_table, own_index, 0, keepdims=False)
    same_dest = own_dest[:, None] == own_dest[None, :]
    rank_own = jnp.sum(jnp.tril(same_dest, -1).astype(jnp.int32), axis=1)
    buf_ssm = (
        jnp.zeros((inst_count, capacity) + send_ssm.shape[1:], send_ssm.dtype)
        .at[own_dest, rank_own]
        .set(send_ssm)
    )
    buf_conv = (
        jnp.zeros((inst_count, capacity) + send_conv.shape[1:], send_conv.dtype)
        .at[own_dest, rank_own]
        .set(send_conv)
    )
    got_ssm, got_conv = (
        lax.all_to_all(buf_ssm, "inst", split_axis=0, concat_axis=0, tiled=True),
        lax.all_to_all(buf_conv, "inst", split_axis=0, concat_axis=0, tiled=True),
    )
    hit_grid = arriving.reshape(inst_count, migrate)
    rank_grid = jnp.cumsum(hit_grid.astype(jnp.int32), axis=1) - 1
    column = jnp.where(hit_grid, rank_grid, capacity)
    source = jnp.broadcast_to(
        jnp.arange(inst_count, dtype=jnp.int32)[:, None], (inst_count, migrate)
    )
    target_grid = (
        jnp.full((inst_count, capacity), slot_count, jnp.int32)
        .at[source, column]
        .set(target_all.reshape(inst_count, migrate), mode="drop")
    )
    flat_target = target_grid.reshape(-1)
    moved_ssm = ssm_state.at[flat_target].set(
        got_ssm.reshape((-1,) + ssm_state.shape[1:]), mode="drop"
    )
    moved_conv = conv_state.at[flat_target].set(
        got_conv.reshape((-1,) + conv_state.shape[1:]), mode="drop"
    )
    steps = x_new.shape[0]
    rank_width = dt_weight.shape[0]
    state_width = a_log.shape[0]
    history = moved_conv
    conv_list = []
    for step_index in range(steps):
        window = jnp.concatenate([history, x_new[step_index][:, None, :]], axis=1)
        conv_list.append(convolve(window, conv_weight, conv_bias))
        history = window[:, 1:, :]
    hidden = moved_ssm.astype(jnp.float32)
    decay_rate = -jnp.exp(a_log)
    results = []
    for step_index in range(steps):
        conv_out = conv_list[step_index]
        partial_sum = jnp.dot(
            conv_out.astype(jnp.bfloat16), proj_weight, preferred_element_type=jnp.float32
        )
        summed = lax.psum(partial_sum, "tp")
        dt_raw = summed[:, :rank_width]
        b_part = summed[:, rank_width : rank_width + state_width]
        c_part = summed[:, rank_width + state_width :]
        normed = (
            dt_raw * lax.rsqrt(jnp.mean(dt_raw * dt_raw, axis=1, keepdims=True) + 1e-06)
        ).astype(jnp.bfloat16)
        step_size = jax.nn.softplus(
            jnp.dot(normed, dt_weight, preferred_element_type=jnp.float32) + dt_bias
        )
        hidden = (
            jnp.exp(step_size[:, None, :] * decay_rate[None, :, :]) * hidden
            + (step_size * conv_out)[:, None, :] * b_part[:, :, None]
        )
        readout = jnp.sum(c_part[:, :, None] * hidden, axis=1) + skip_gain * conv_out
        results.append(
            (readout * jax.nn.silu(z_new[step_index].astype(jnp.float32))).astype(jnp.bfloat16)
        )
    return (jnp.stack(results), hidden.astype(jnp.bfloat16), history)


def solution(mesh):
    return jax.shard_map(
        local,
        mesh=mesh,
        in_specs=(
            P(None, ("groups", "inst"), "tp"),
            P(None, ("groups", "inst"), "tp"),
            P(("groups", "inst"), None, "tp"),
            P(("groups", "inst"), None, "tp"),
            P(None, "tp"),
            P("tp"),
            P("tp", None),
            P(None, "tp"),
            P("tp"),
            P(None, "tp"),
            P("tp"),
            P(("groups", "inst"), None),
            P("groups", None),
            P(("groups", "inst"), None),
        ),
        out_specs=(
            P(None, ("groups", "inst"), "tp"),
            P(("groups", "inst"), None, "tp"),
            P(("groups", "inst"), None, "tp"),
        ),
        check_vma=False,
    )
```

profile of v0, /device:TPU:0, one launch (start us, length us, event | category | flops | bytes accessed | tf_op | source)
XLA Modules:
  0.0 144.2 jit_solution(3335983464978425284)
XLA Ops:
  7.2 1.3 copy.55
  8.5 6.3 %copy.54 = bf16[48,16,4096]{2,1,0:T(8,128)(2,1)} copy(bf16[48,16,4096]{2,1,0:T(8,128)(2,1)} %param.16) | data formatting | bytes 12582912
  15.0 1.7 %gather_fusion.1 = bf16[12,3,4096]{2,0,1:T(8,128)(2,1)S(1)} fusion(bf16[48,3,4096]{2,0,1:T(8,128)(2,1)S(1)} %copy.55, s32[1024]{0:T(1024)S(1)} %pad_clamp_fusion), kind=kCustom, calls=%fused_computation.1 | custom fusion | bytes 589872 | tf_op jit(solution)/shard_map/jit(_take)/gather | solution.py:39
  17.3 1.1 scatter_fusion.1
  18.4 1.1 copy.30
  19.5 4.2 %all-to-all-start = ((bf16[4,4,3,4096]{3,1,2,0:T(4,128)(2,1)}), bf16[4,4,3,4096]{3,1,2,0:T(4,128)(2,1)}, u32[]{:S(2)}, u32[]{:S(2)}) async-start(bf16[4,4,3,4096]{3,1,2,0:T(4,128)(2,1)} %copy.30), calls=%async_computation | async-start | bytes 786432 | tf_op jit(solution)/shard_map/all_to_all | solution.py:56
  26.3 4.6 %gather_fusion.2 = bf16[12,16,4096]{2,1,0:T(8,128)(2,1)} fusion(bf16[48,16,4096]{2,1,0:T(8,128)(2,1)} %copy.54, s32[1024]{0:T(1024)S(1)} %pad_clamp_fusion), kind=kCustom, calls=%fused_computation.2 | custom fusion | bytes 3145776 | tf_op jit(solution)/shard_map/jit(_take)/gather | solution.py:38
  30.9 1.7 %broadcast_select_fusion = bf16[12,16,4096]{2,1,0:T(8,128)(2,1)S(1)} fusion(bf16[12,16,4096]{2,1,0:T(8,128)(2,1)} %gather_fusion.2, pred[12]{0:T(512)(128)(4,1)S(1)} %compare_and_fusion), kind=kLoop, calls=%fused_computation.27 | loop fusion | flops 786432 | bytes 3145740 | tf_op jit(solution)/shard_map/jit(_take)/select_n | solution.py:38
  34.2 1.3 reshape.248
  35.5 4.4 %scatter_fusion = s32[4,4]{1,0:T(4,128)S(1)} fusion(s32[4,4]{1,0:T(4,128)S(1)} %broadcast.258, s32[48]{0:T(128)S(1)} %reshape.246, s32[48]{0:T(128)} %reshape.248), kind=kCustom, calls=%fused_computation.3 | custom fusion | bytes 960 | tf_op jit(solution)/shard_map/scatter | solution.py:67
  40.5 1.5 %broadcast_in_dim.52 = bf16[4,4,16,4096]{3,2,1,0:T(8,128)(2,1)} broadcast(bf16[]{:T(256)} %constant.93.clone.1), dimensions={} | broadcast | bytes 2097154 | tf_op jit(solution)/shard_map/broadcast_in_dim | solution.py:45
  42.0 5.1 %scatter_fusion.3 = bf16[4,4,16,4096]{3,2,1,0:T(8,128)(2,1)} fusion(bf16[4,4,16,4096]{3,2,1,0:T(8,128)(2,1)} %broadcast_in_dim.52, s32[12]{0:T(128)S(1)} %fusion.40, bf16[12,16,4096]{2,1,0:T(8,128)(2,1)S(1)} %broadcast_select_fusion), kind=kCustom, calls=%fused_computation.6 | custom fusion | bytes 4718688 | tf_op jit(solution)/shard_map/scatter | solution.py:47
  47.1 4.5 %all-to-all-start.1 = ((bf16[4,4,16,4096]{3,2,1,0:T(8,128)(2,1)}), bf16[4,4,16,4096]{3,2,1,0:T(8,128)(2,1)}, u32[]{:S(2)}, u32[]{:S(2)}) async-start(bf16[4,4,16,4096]{3,2,1,0:T(8,128)(2,1)} %scatter_fusion.3), calls=%async_computation.1 | async-start | bytes 4194304 | tf_op jit(solution)/shard_map/all_to_all | solution.py:55
  51.8 1.2 copy.31
  53.1 6.7 %scatter_fusion.2 = bf16[48,3,4096]{2,0,1:T(8,128)(2,1)S(1)} fusion(bf16[48,3,4096]{2,0,1:T(8,128)(2,1)S(1)} %copy.55, s32[16]{0:T(128)S(1)} %fusion.38, bf16[16,3,4096]{2,0,1:T(8,128)(2,1)S(1)} %reshape.262), kind=kCustom, calls=%fused_computation.5 | custom fusion | bytes 1179712 | tf_op jit(solution)/shard_map/scatter | solution.py:73
  60.7 5.3 %fusion.23 = f32[48,544]{1,0:T(8,128)} fusion(bf16[4096,544]{0,1:T(8,128)(2,1)} %param.20, f32[4096,48]{0,1:T(8,128)S(1)} %get-tuple-element.5, f32[4096]{0:T(1024)S(1)} %copy-done.14), kind=kOutput, calls=%fused_computation.58 | convolution fusion | flops 215089152 | bytes 5363712 | tf_op jit(solution)/shard_map/dot_general | solution.py:90
  66.0 2.1 %fusion.21 = f32[48,544]{1,0:T(8,128)} fusion(bf16[4096,544]{0,1:T(8,128)(2,1)S(1)} %bitcast.101, f32[4096,48]{0,1:T(8,128)S(1)} %get-tuple-element.6, f32[4096]{0:T(1024)S(1)} %copy-done.14), kind=kOutput, calls=%fused_computation.55 | convolution fusion | flops 215089152 | bytes 5363712 | tf_op jit(solution)/shard_map/dot_general | solution.py:90
  68.2 1.1 fusion.3
  69.3 37.3 %all-reduce.3.cloned.1.call-done = (f32[48,544]{1,0:T(8,128)}, f32[48,544]{1,0:T(8,128)}) async-done(((f32[48,544]{1,0:T(8,128)}, f32[48,544]{1,0:T(8,128)}), (f32[48,544]{1,0:T(8,128)}, f32[48,544]{1,0:T(8,128)})) %all-reduce.3.cloned.1.call-update) | async-done | bytes 208912 | tf_op jit(solution)/shard_map/psum | solution.py:93
  106.6 1.2 multiply_reduce_fusion.4
  108.8 3.4 %compare_select_fusion.1 = f32[48,4096]{1,0:T(8,128)S(1)} fusion(bf16[512,4096]{1,0:T(8,128)(2,1)} %param.21, f32[4096]{0:T(1024)S(1)} %copy-done.13, f32[48,544]{1,0:T(8,128)} %get-tuple-element.9, f32[48]{0:T(128)S(1)} %add_rsqrt_fusion.1), kind=kOutput, calls=%fused_computation.18 | convolution fusion | flops 202752000 | bytes 5095616 | tf_op jit(solution)/shard_map/dot_general | solution.py:101
  112.3 2.7 %fusion.43 = (f32[48,4096]{1,0:T(8,128)S(1)}, f32[48,4096]{1,0:T(8,128)}, f32[48,4096]{1,0:T(8,128)}) fusion(f32[4096,48]{0,1:T(8,128)S(1)} %copy-done.5, f32[4096]{0:T(1024)S(1)} %copy-done.15, f32[48,4096]{1,0:T(8,128)S(1)} %compare_select_fusion.1, f32[4096,48]{0,1:T(8,128)S(1)} %copy-done.3, f32[4096]{0:T(1024)S(1)} %copy-done.13, ...), kind=kOutput, calls=%fused_computation.112 | convolution fusion | flops 205111296 | bytes 9044480 | tf_op jit(solution)/shard_map/dot_general | solution.py:101
  114.9 5.8 %scatter_fusion.4 = bf16[48,16,4096]{2,1,0:T(8,128)(2,1)} fusion(bf16[48,16,4096]{2,1,0:T(8,128)(2,1)} %copy.54, s32[16]{0:T(128)S(1)} %fusion.38, bf16[16,16,4096]{2,1,0:T(8,128)(2,1)} %bitcast.16), kind=kCustom, calls=%fused_computation.7 | custom fusion | bytes 6291520 | tf_op jit(solution)/shard_map/scatter | solution.py:70
  120.7 14.7 %multiply_reduce_fusion.1 = (f32[48,4096]{1,0:T(8,128)S(1)}, f32[48,4096]{1,0:T(8,128)S(1)}, bf16[48,16,4096]{2,1,0:T(8,128)(2,1)}) fusion(bf16[48,16,4096]{2,1,0:T(8,128)(2,1)} %scatter_fusion.4, f32[48,16]{1,0:T(8,128)S(1)} %get-tuple-element.27, f32[48,4096]{1,0:T(8,128)} %get-tuple-element.23, f32[16,4096]{1,0:T(8,128)S(1)} %copy-done.7, ...), kind=kLoop, calls=%fused_computation.10 | loop fusion | flops 43646976 | bytes 17575936 | tf_op jit(solution)/shard_map/reduce_sum | solution.py:107
  (90 shorter events, 9.4 us)
Async XLA Ops:
  7.2 18.2 %copy-start = (s32[1,12]{1,0:T(1,128)S(1)}, s32[1,12]{1,0:T(1,128)}, u32[]{:S(2)}) copy-start(s32[1,12]{1,0:T(1,128)} %param.27) | copy-start | bytes 148
  8.5 6.3 %copy-start.22 = (s32[1,12]{1,0:T(1,128)S(1)}, s32[1,12]{1,0:T(1,128)}, u32[]{:S(2)}) copy-start(s32[1,12]{1,0:T(1,128)} %param.25) | copy-start | bytes 148
  8.5 6.3 %copy-start.20 = (s32[4,12]{1,0:T(4,128)S(1)}, s32[4,12]{1,0:T(4,128)}, u32[]{:S(2)}) copy-start(s32[4,12]{1,0:T(4,128)} %param.26) | copy-start | bytes 580
  19.5 27.6 %all-to-all-start = ((bf16[4,4,3,4096]{3,1,2,0:T(4,128)(2,1)}), bf16[4,4,3,4096]{3,1,2,0:T(4,128)(2,1)}, u32[]{:S(2)}, u32[]{:S(2)}) async-start(bf16[4,4,3,4096]{3,1,2,0:T(4,128)(2,1)} %copy.30), calls=%async_computation | async-start | bytes 786432 | tf_op jit(solution)/shard_map/all_to_all | solution.py:56
  30.9 3.2 %copy-start.18 = (s32[4,12]{1,0:T(4,128)S(1)}, s32[4,12]{1,0:T(4,128)}, u32[]{:S(2)}) copy-start(s32[4,12]{1,0:T(4,128)} %reduce_window_sum.18) | copy-start | bytes 580
  40.5 6.6 %copy-start.21 = (s32[16,1]{0,1:T(1,128)S(1)}, s32[16,1]{0,1:T(1,128)}, u32[]{:S(2)}) copy-start(s32[16,1]{0,1:T(1,128)} %reshape.216) | copy-start | bytes 196
  47.1 67.8 %all-to-all-start.1 = ((bf16[4,4,16,4096]{3,2,1,0:T(8,128)(2,1)}), bf16[4,4,16,4096]{3,2,1,0:T(8,128)(2,1)}, u32[]{:S(2)}, u32[]{:S(2)}) async-start(bf16[4,4,16,4096]{3,2,1,0:T(8,128)(2,1)} %scatter_fusion.3), calls=%async_computation.1 | async-start | bytes 4194304 | tf_op jit(solution)/shard_map/all_to_all | solution.py:55
  51.6 55.0 %all-reduce.3.cloned.1.call-start = ((), (), s32[]{:S(2)}) async-start(), calls=%async_computation.2 | async-start | bytes 491520 | tf_op jit(solution)/shard_map/psum | solution.py:93
  53.1 6.8 %copy-start.12 = (f32[4,4096]{1,0:T(4,128)S(1)}, f32[4,4096]{1,0:T(4,128)}, u32[]{:S(2)}) copy-start(f32[4,4096]{1,0:T(4,128)} %param.18) | copy-start | bytes 196612
  59.8 6.2 %slice-start = ((s8[4456448]{0:T(1024)(128)(4,1)}), s8[4194304]{0:T(1024)(128)(4,1)S(1)}, s32[]{:S(2)}) async-start(s8[4456448]{0:T(1024)(128)(4,1)} %bitcast.100), calls=%async_computation.3 | async-start | bytes 8388608
  59.9 6.0 %slice-start.1 = ((s8[4456448]{0:T(1024)(128)(4,1)}), s8[262144]{0:T(1024)(128)(4,1)S(1)}, s32[]{:S(2)}) async-start(s8[4456448]{0:T(1024)(128)(4,1)} %bitcast.100), calls=%async_computation.4 | async-start | bytes 524288
  60.6 5.4 %copy-start.2 = (f32[4096,48]{0,1:T(8,128)}, f32[4096,48]{0,1:T(8,128)S(1)}, u32[]{:S(2)}) copy-start(f32[4096,48]{0,1:T(8,128)S(1)} %get-tuple-element.5) | copy-start | bytes 2359300
  60.6 5.4 %copy-start.4 = (f32[4096,48]{0,1:T(8,128)}, f32[4096,48]{0,1:T(8,128)S(1)}, u32[]{:S(2)}) copy-start(f32[4096,48]{0,1:T(8,128)S(1)} %get-tuple-element.6) | copy-start | bytes 2359300
  68.1 40.7 %copy-start.13 = (f32[4096]{0:T(1024)S(1)}, f32[4096]{0:T(1024)}, u32[]{:S(2)}) copy-start(f32[4096]{0:T(1024)} %param.22) | copy-start | bytes 49156
  68.2 44.1 %copy-start.5 = (f32[4096,48]{0,1:T(8,128)S(1)}, f32[4096,48]{0,1:T(8,128)}, u32[]{:S(2)}) copy-start(f32[4096,48]{0,1:T(8,128)} %copy-done.4) | copy-start | bytes 2359300
  69.3 42.9 %copy-start.3 = (f32[4096,48]{0,1:T(8,128)S(1)}, f32[4096,48]{0,1:T(8,128)}, u32[]{:S(2)}) copy-start(f32[4096,48]{0,1:T(8,128)} %copy-done.2) | copy-start | bytes 2359300
  69.3 42.9 %copy-start.15 = (f32[4096]{0:T(1024)S(1)}, f32[4096]{0:T(1024)}, u32[]{:S(2)}) copy-start(f32[4096]{0:T(1024)} %param.19) | copy-start | bytes 49156
  106.6 5.7 %copy-start.1 = (bf16[512,4096]{1,0:T(8,128)(2,1)S(1)}, bf16[512,4096]{1,0:T(8,128)(2,1)}, u32[]{:S(2)}) copy-start(bf16[512,4096]{1,0:T(8,128)(2,1)} %param.21) | copy-start | bytes 12582916
  106.6 5.7 %copy-start.11 = (f32[48,544]{1,0:T(8,128)S(1)}, f32[48,544]{1,0:T(8,128)}, u32[]{:S(2)}) copy-start(f32[48,544]{1,0:T(8,128)} %get-tuple-element.10) | copy-start | bytes 313348
  114.9 5.8 %copy-start.7 = (f32[16,4096]{1,0:T(8,128)S(1)}, f32[16,4096]{1,0:T(8,128)}, u32[]{:S(2)}) copy-start(f32[16,4096]{1,0:T(8,128)} %exponential_negate_fusion) | copy-start | bytes 786436
  120.7 14.8 %copy-start.6 = (f32[4096,48]{0,1:T(8,128)S(1)}, f32[4096,48]{0,1:T(8,128)}, u32[]{:S(2)}) copy-start(f32[4096,48]{0,1:T(8,128)} %copy-done.4) | copy-start | bytes 2359300
  120.7 14.8 %copy-start.8 = (bf16[2,48,4096]{2,1,0:T(8,128)(2,1)S(1)}, bf16[2,48,4096]{2,1,0:T(8,128)(2,1)}, u32[]{:S(2)}) copy-start(bf16[2,48,4096]{2,1,0:T(8,128)(2,1)} %param.15) | copy-start | bytes 2359300
  120.7 14.8 %copy-start.16 = (f32[4096]{0:T(1024)S(1)}, f32[4096]{0:T(1024)}, u32[]{:S(2)}) copy-start(f32[4096]{0:T(1024)} %param.19) | copy-start | bytes 49156
  120.7 14.8 %copy-start.17 = (f32[4096]{0:T(1024)S(1)}, f32[4096]{0:T(1024)}, u32[]{:S(2)}) copy-start(f32[4096]{0:T(1024)} %param.24) | copy-start | bytes 49156
  (4 other events, 6.9 us)
Sparse Core Ops, SparseCore 0:
  68.3 38.2 all-reduce.2
where the time goes:
time: 145 us; the launch traced here: 144 us
  local copies, waits for them, and re-layouts  45.5 us (31%)
  waiting for transfers between devices  37.3 us (26%)
  other arithmetic  24.5 us (17%)
  between operations  14.4 us (10%)
  matrix products  13.5 us (9%)
  starting transfers between devices  8.91 us (6%)
    psum x1, waiting for transfers between devices, local(): summed = lax.psum(partial_sum, 'tp')  37.3 us
    reduce_sum x1, other arithmetic, local(): jnp.sum(c_part[:, :, None] * hidden, axis=1) + skip_gain * conv_out  14.7 us
    unnamed x52, local copies, waits for them, and re-layouts  7.71 us
    dot_general x2, matrix products, local(): jnp.dot(conv_out.astype(jnp.bfloat16), proj_weight, preferred_element_typ...  7.44 us
    scatter x1, local copies, waits for them, and re-layouts, local(): conv_state.at[flat_target]  6.68 us
    dot_general x2, matrix products, local(): jnp.dot(normed, dt_weight, preferred_element_type=jnp.float32) + dt_bias  6.03 us
    scatter x1, local copies, waits for them, and re-layouts, local(): ssm_state.at[flat_target]  5.76 us
    scatter x1, local copies, waits for them, and re-layouts, local(): buf_ssm = jnp.zeros((inst_count, capacity) + send_ssm.shape[1:], send_ssm...  5.09 us
  transfers between devices with their start and end apart: 3, of which 1 were waited for; matrix products, arithmetic and copies ran while one was open for 34% of the time, Pallas kernels for 0%

commit v1 on v0

v1 whole, which is shorter than its diff:
```python
import functools
import math

import jax
import jax.numpy as jnp
from jax import lax
from jax.experimental import pallas as pl
from jax.experimental.pallas import tpu as pltpu
from jax.sharding import PartitionSpec as P

F32 = jnp.float32
BF16 = jnp.bfloat16
LANES = 128
LOG2E = math.log2(math.e)
MIB = 1 << 20


def iota(shape, dim):
    return lax.broadcasted_iota(jnp.int32, shape, dim)


def silu(value):
    return value / (1.0 + jnp.exp(-value))


def gather_kernel(n, cap, chunks, leave, dest, land, own_ref, conv, ssm, *rest):
    peers = n - 1
    conv_send = rest[:peers]
    ssm_send = rest[peers : 2 * peers]
    land_tab, stay_tab, leave_tab, flags, sems = rest[2 * peers :]
    mig = leave.shape[1]
    slots = ssm.shape[0]
    taps = conv.shape[0]
    width = conv.shape[2] // chunks
    own = own_ref[0]

    def clear(i, _):
        leave_tab[i] = -1
        land_tab[i] = -1
        return 0

    lax.fori_loop(0, n * cap, clear, 0, unroll=True)

    for pos in range(mig):
        peer = dest[own, pos] ^ own
        rank = 0
        for earlier in range(pos):
            rank = rank + jnp.where(dest[own, earlier] ^ own == peer, 1, 0)
        leave_tab[peer * cap + rank] = leave[0, pos]

    def copy(k, s, slot):
        return pltpu.make_async_copy(ssm.at[slot], ssm_send[k - 1].at[s], sems.at[k - 1, s])

    for k in range(1, n):
        for s in range(cap):
            slot = leave_tab[k * cap + s]

            @pl.when(slot >= 0)
            def _():
                copy(k, s, slot).start()

    rows = chunks * taps * cap
    row = iota((rows, taps * slots), 0)
    col = iota((rows, taps * slots), 1)
    place = lax.rem(row, cap)
    tap = lax.rem(lax.div(row, cap), taps)
    chunk = lax.div(row, taps * cap)
    table = conv[...].reshape(taps * slots, conv.shape[2])
    picks = []
    for k in range(1, n):
        source = jnp.full(row.shape, -1, jnp.int32)
        for s in range(cap):
            slot = leave_tab[k * cap + s]
            source = jnp.where((place == s) & (slot >= 0), tap * slots + slot, source)
        picks.append(source == col)
    for k in range(1, n):
        total = jnp.zeros((rows, width), F32)
        for q in range(chunks):
            pick = jnp.where(picks[k - 1] & (chunk == q), 1.0, 0.0).astype(BF16)
            total += jnp.dot(pick, table[:, q * width : (q + 1) * width], preferred_element_type=F32)
        conv_send[k - 1][...] = total.astype(BF16)

    def arrivals(source, rank):
        def one(pos, carry):
            rank, place = carry
            hit = dest[source, pos] == own

            @pl.when(hit)
            def _():
                land_tab[(source ^ own) * cap + place] = land[0, rank]

            step = jnp.where(hit, 1, 0)
            return rank + step, place + step

        return lax.fori_loop(0, mig, one, (rank, 0))[0]

    lax.fori_loop(0, n, arrivals, 0)

    def unset(i, _):
        flags[i] = 0
        return 0

    lax.fori_loop(0, slots, unset, 0, unroll=8)
    for pos in range(mig):
        flags[leave[0, pos]] = 1

    def staying(slot, count):
        @pl.when(flags[slot] == 0)
        def _():
            stay_tab[count] = slot

        return count + 1 - flags[slot]

    lax.fori_loop(0, slots, staying, 0)

    for k in range(1, n):
        for s in range(cap):
            slot = leave_tab[k * cap + s]

            @pl.when(slot >= 0)
            def _():
                copy(k, s, slot).wait()


def project_kernel(n, cap, land_tab, *rest):
    peers = n - 1
    got = rest[:peers]
    conv, x_new, weight, bias, proj = rest[peers : peers + 5]
    conv_out, new_conv, own_sum, send_sum, total = rest[peers + 5 :]
    q = pl.program_id(0)
    taps, slots, width = conv.shape
    rows = got[0].shape[0]
    cols = proj.shape[0]

    col = iota((1, peers * rows), 1)
    inner = lax.rem(col, rows)
    target = jnp.full(col.shape, -1, jnp.int32)
    slot_row = iota((slots, 1), 0)
    arrived = jnp.zeros((slots, 1), jnp.bool_)
    for k in range(1, n):
        for s in range(cap):
            slot = land_tab[k * cap + s]
            target = jnp.where((lax.div(col, rows) == k - 1) & (lax.rem(inner, cap) == s), slot, target)
            arrived = arrived | (slot_row == slot)
    tap = lax.rem(lax.div(inner, cap), taps)
    target = jnp.where(lax.div(inner, taps * cap) == q, target, -1)
    grid_row = iota((slots, peers * rows), 0)
    incoming = jnp.concatenate([g[...] for g in got], axis=0)
    history = []
    for j in range(taps):
        pick = jnp.where(grid_row == jnp.where(tap == j, target, -1), 1.0, 0.0).astype(BF16)
        moved = jnp.dot(pick, incoming, preferred_element_type=F32)
        history.append(jnp.where(arrived, moved, conv[j].astype(F32)))
    new_conv[0] = history[taps - 1].astype(BF16)
    new_conv[1] = x_new[0]
    new_conv[2] = x_new[1]
    window = history + [x_new[0].astype(F32), x_new[1].astype(F32)]
    halves = []
    for t in range(2):
        value = window[t] * weight[0:1, :]
        for j in range(1, taps + 1):
            value += window[t + j] * weight[j : j + 1, :]
        value = silu(value + bias[...])
        conv_out[t] = value
        halves.append(value.astype(BF16))
    part = lax.dot_general(
        jnp.concatenate(halves, axis=0), proj[...], (((1,), (1,)), ((), ())), preferred_element_type=F32
    )

    @pl.when(q == 0)
    def _():
        total[...] = jnp.zeros_like(total)

    total[:, :cols] += part

    @pl.when(q == pl.num_programs(0) - 1)
    def _():
        rank = total.shape[1] - LANES
        own_sum[...] = total[...]
        send_sum[:, :rank] = total[:, :rank].astype(BF16)
        tail = total[:, rank:]
        high = tail.astype(BF16).astype(F32)
        send_sum[:, rank:] = (high + pltpu.roll(tail - high, cols - rank, 1)).astype(BF16)


def spread(values, lane, states):
    rows = values.shape[0]
    wide = jnp.broadcast_to(values[:, None, :], (rows, states, LANES))
    keep = iota(wide.shape, 2) == iota(wide.shape, 1) + lane
    wide = jnp.where(keep, wide, 0.0).reshape(rows * states, LANES)
    high = wide.astype(BF16)
    low = (wide - high.astype(F32)).astype(BF16)
    ones = jnp.ones((LANES, LANES), BF16)
    both = jnp.dot(high, ones, preferred_element_type=F32) + jnp.dot(low, ones, preferred_element_type=F32)
    return both.reshape(rows, states, LANES)


def advance(hidden, rate, steps):
    sums = []
    for size, drive, b_part, c_part in steps:
        hidden = jnp.exp2(size * rate) * hidden + drive * b_part
        sums.append(jnp.sum(c_part * hidden, axis=0, keepdims=True))
    return hidden, sums


def wide(tile, lanes):
    return jnp.concatenate([tile] * (lanes // LANES), axis=1)


def stay_kernel(n, tps, cap, stays, land_tab, stay_tab, own_sum, *rest):
    got = rest[: tps - 1]
    dt_weight, dt_bias, a_log, skip, conv_out, z_new, ssm = rest[tps - 1 : tps + 6]
    new_ssm, out, size_m, drive_m, skip_m, gate_m, b_m, c_m = rest[tps + 6 : tps + 14]
    normed, b_all, c_all, size_s, drive_s, skip_s, gate_s, read_s = rest[tps + 14 :]
    rank = dt_weight.shape[0]
    states, width = a_log.shape
    slots = ssm.shape[0]
    movers = (n - 1) * cap

    @pl.when(pl.program_id(0) == 0)
    def _():
        raw = own_sum[:, :rank]
        tail = own_sum[:, rank:]
        for g in got:
            raw += g[:, :rank].astype(F32)
            piece = g[:, rank:].astype(F32)
            tail += piece + pltpu.roll(piece, LANES - 2 * states, 1)
        scale = lax.rsqrt(jnp.mean(raw * raw, axis=1, keepdims=True) + 1e-06)
        normed[...] = (raw * scale).astype(BF16)
        b_all[...] = spread(tail, 0, states)
        c_all[...] = spread(tail, states, states)
        for t in range(2):
            for k in range(1, n):
                for s in range(cap):
                    slot = jnp.maximum(land_tab[k * cap + s], 0)
                    at = t * movers + (k - 1) * cap + s
                    b_m[at] = b_all[t * slots + slot]
                    c_m[at] = c_all[t * slots + slot]

    pre = jnp.dot(normed[...], dt_weight[...], preferred_element_type=F32) + dt_bias[...]
    size = jnp.maximum(pre, 0.0) + jnp.log1p(jnp.exp(-jnp.abs(pre)))
    conv = conv_out[...].reshape(2 * slots, width)
    gate = silu(z_new[...].reshape(2 * slots, width).astype(F32))
    size_s[...] = size
    drive_s[...] = size * conv
    skip_s[...] = skip[...] * conv
    gate_s[...] = gate
    rate = -LOG2E * jnp.exp(a_log[...])

    def one(i, _):
        slot = stay_tab[i]
        steps = []
        for t in range(2):
            at = t * slots + slot
            steps.append(
                (
                    size_s[pl.ds(at, 1), :],
                    drive_s[pl.ds(at, 1), :],
                    wide(b_all[at], width),
                    wide(c_all[at], width),
                )
            )
        hidden, sums = advance(ssm[slot].astype(F32), rate, steps)
        new_ssm[slot] = hidden.astype(BF16)
        for t in range(2):
            read_s[pl.ds(t * slots + slot, 1), :] = sums[t]
        return 0

    lax.fori_loop(0, stays, one, 0)
    done = (read_s[...] + skip_s[...]) * gate_s[...]
    out[...] = done.reshape(2, slots, width).astype(BF16)
    for t in range(2):
        for k in range(1, n):
            for s in range(cap):
                from_row = pl.ds(t * slots + jnp.maximum(land_tab[k * cap + s], 0), 1)
                at = t * movers + (k - 1) * cap + s
                for ref, source in ((size_m, size_s), (drive_m, drive_s), (skip_m, skip_s), (gate_m, gate_s)):
                    ref[at : at + 1, :] = source[from_row, :]


def arrive_kernel(n, cap, land_tab, *rest):
    peers = n - 1
    got = rest[:peers]
    a_log, size_m, drive_m, skip_m, gate_m, b_m, c_m, out_in, _ = rest[peers : peers + 9]
    out, new_ssm, fresh, read_s, sems = rest[peers + 9 :]
    step = pl.program_id(0)
    states, width = a_log.shape
    movers = peers * cap
    slots = out.shape[1]
    rate = -LOG2E * jnp.exp(a_log[...])

    def copy(i, place):
        lanes = pl.ds(pl.multiple_of(place * width, width), width)
        return pltpu.make_async_copy(
            fresh.at[place, i], new_ssm.at[land_tab[cap + i], :, lanes], sems.at[place, i]
        )

    read_s[...] = jnp.zeros_like(read_s)
    for k in range(1, n):
        for s in range(cap):
            i = (k - 1) * cap + s
            steps = []
            for t in range(2):
                at = t * movers + i
                steps.append(
                    (
                        size_m[at : at + 1, :],
                        drive_m[at : at + 1, :],
                        wide(b_m[at], width),
                        wide(c_m[at], width),
                    )
                )
            hidden, sums = advance(got[k - 1][s].astype(F32), rate, steps)
            fresh[step, i] = hidden.astype(BF16)

            @pl.when(land_tab[cap + i] >= 0)
            def _():
                copy(i, step).start()

            for t in range(2):
                at = t * movers + i
                done = (sums[t] + skip_m[at : at + 1, :]) * gate_m[at : at + 1, :]
                read_s[t, i : i + 1, :] = done
    pad = read_s.shape[1]
    row = iota((slots, pad), 0)
    col = iota((1, pad), 1)
    target = jnp.full(col.shape, -1, jnp.int32)
    arrived = jnp.zeros((slots, 1), jnp.bool_)
    slot_row = iota((slots, 1), 0)
    for i in range(movers):
        slot = land_tab[cap + i]
        target = jnp.where(col == i, slot, target)
        arrived = arrived | (slot_row == slot)
    pick = jnp.where(row == target, 1.0, 0.0).astype(BF16)
    for t in range(2):
        placed = jnp.dot(pick, read_s[t].astype(BF16), preferred_element_type=F32)
        out[t] = jnp.where(arrived, placed, out_in[t].astype(F32)).astype(BF16)

    @pl.when(step == pl.num_programs(0) - 1)
    def _():
        for place in range(fresh.shape[0]):
            for i in range(movers):

                @pl.when(land_tab[cap + i] >= 0)
                def _():
                    copy(i, place).wait()


def exchange(value, axis, k, n):
    return lax.ppermute(value, axis, [(i, i ^ k) for i in range(n)])


def spec(shape, index=None):
    if index is None:
        return pl.BlockSpec(shape, lambda i: (0,) * len(shape))
    return pl.BlockSpec(shape, index)


def last(*lead):
    return pl.BlockSpec(lead, lambda i: (0,) * (len(lead) - 1) + (i,))


def params(mib):
    return pltpu.CompilerParams(vmem_limit_bytes=mib * MIB)


def local(
    n,
    tps,
    x_new,
    z_new,
    ssm_state,
    conv_state,
    conv_weight,
    conv_bias,
    proj_weight,
    dt_weight,
    dt_bias,
    a_log,
    skip_gain,
    leave_slot,
    dest_table,
    land_slot,
):
    slots, states, channels = ssm_state.shape
    mig = leave_slot.shape[1]
    taps = conv_state.shape[1]
    rank = dt_weight.shape[0]
    peers = n - 1
    cap = max(2, (mig + n - 2) // (n - 1))
    movers = peers * cap
    stays = slots - mig
    chunks = 16 // math.gcd(16, taps * cap)
    rows = chunks * taps * cap
    width = channels // chunks
    smem = pl.BlockSpec(memory_space=pltpu.SMEM)
    vmem = pl.BlockSpec(memory_space=pltpu.VMEM)
    hbm = pl.BlockSpec(memory_space=pl.ANY)
    shape = jax.ShapeDtypeStruct
    own = lax.axis_index("inst").astype(jnp.int32).reshape(1)
    conv_t = jnp.transpose(conv_state, (1, 0, 2))
    proj_t = proj_weight.T
    cols = proj_t.shape[0]
    padded = rank + LANES
    bias_row = conv_bias.reshape(1, channels)
    dt_bias_row = dt_bias.reshape(1, channels)
    skip_row = skip_gain.reshape(1, channels)

    with jax.named_scope("gather_leaving"):
        sent = pl.pallas_call(
            functools.partial(gather_kernel, n, cap, chunks),
            out_shape=[shape((rows, width), BF16)] * peers
            + [shape((cap, states, channels), BF16)] * peers
            + [shape((n * cap,), jnp.int32), shape((slots,), jnp.int32)],
            in_specs=[smem] * 4 + [vmem, hbm],
            out_specs=[vmem] * peers + [hbm] * peers + [smem, smem],
            scratch_shapes=[
                pltpu.SMEM((n * cap,), jnp.int32),
                pltpu.SMEM((slots,), jnp.int32),
                pltpu.SemaphoreType.DMA((peers, cap)),
            ],
            compiler_params=params(24),
        )(leave_slot, dest_table, land_slot, own, conv_t, ssm_state)
    conv_sent, ssm_sent = sent[:peers], sent[peers : 2 * peers]
    land_tab, stay_tab = sent[2 * peers :]

    order = sorted(range(1, n), key=lambda k: -k)
    conv_got, ssm_got = {}, {}
    for k in order:
        conv_got[k] = exchange(conv_sent[k - 1], "inst", k, n)
    for k in order:
        ssm_got[k] = exchange(ssm_sent[k - 1], "inst", k, n)

    with jax.named_scope("project"):
        conv_out, new_conv, own_sum, send_sum = pl.pallas_call(
            functools.partial(project_kernel, n, cap),
            grid=(chunks,),
            out_shape=[
                shape((2, slots, channels), F32),
                shape((taps, slots, channels), BF16),
                shape((2 * slots, padded), F32),
                shape((2 * slots, padded), BF16),
            ],
            in_specs=[smem]
            + [spec((rows, width))] * peers
            + [
                last(taps, slots, width),
                last(2, slots, width),
                last(taps + 1, width),
                last(1, width),
                last(cols, width),
            ],
            out_specs=[
                last(2, slots, width),
                last(taps, slots, width),
                spec((2 * slots, padded)),
                spec((2 * slots, padded)),
            ],
            scratch_shapes=[pltpu.VMEM((2 * slots, padded), F32)],
            compiler_params=params(32),
        )(
            land_tab,
            *[conv_got[k] for k in range(1, n)],
            conv_t,
            x_new,
            conv_weight,
            bias_row,
            proj_t,
        )

    sums_got = [exchange(send_sum, "tp", k, tps) for k in range(tps - 1, 0, -1)]

    step = min(512, channels)
    with jax.named_scope("update_staying"):
        stay_out = pl.pallas_call(
            functools.partial(stay_kernel, n, tps, cap, stays),
            grid=(channels // step,),
            out_shape=[
                shape((slots, states, channels), BF16),
                shape((2, slots, channels), BF16),
                shape((2 * movers, channels), F32),
                shape((2 * movers, channels), F32),
                shape((2 * movers, channels), F32),
                shape((2 * movers, channels), F32),
                shape((2 * movers, states, LANES), F32),
                shape((2 * movers, states, LANES), F32),
            ],
            in_specs=[smem, smem]
            + [spec((2 * slots, padded))] * tps
            + [
                last(rank, step),
                last(1, step),
                last(states, step),
                last(1, step),
                last(2, slots, step),
                last(2, slots, step),
                last(slots, states, step),
            ],
            out_specs=[last(slots, states, step), last(2, slots, step)]
            + [last(2 * movers, step)] * 4
            + [spec((2 * movers, states, LANES))] * 2,
            scratch_shapes=[
                pltpu.VMEM((2 * slots, rank), BF16),
                pltpu.VMEM((2 * slots, states, LANES), F32),
                pltpu.VMEM((2 * slots, states, LANES), F32),
            ]
            + [pltpu.VMEM((2 * slots, step), F32)] * 5,
            compiler_params=params(32),
        )(
            land_tab,
            stay_tab,
            own_sum,
            *sums_got,
            dt_weight,
            dt_bias_row,
            a_log,
            skip_row,
            conv_out,
            z_new,
            ssm_state,
        )
    new_ssm, out_stay, *moving = stay_out

    wide_step = min(1024, channels)
    grid = channels // wide_step
    pad = -(-movers // 16) * 16
    with jax.named_scope("update_arrived"):
        outputs, new_ssm = pl.pallas_call(
            functools.partial(arrive_kernel, n, cap),
            grid=(grid,),
            out_shape=[shape((2, slots, channels), BF16), shape((slots, states, channels), BF16)],
            in_specs=[smem]
            + [last(cap, states, wide_step)] * peers
            + [last(states, wide_step)]
            + [last(2 * movers, wide_step)] * 4
            + [spec((2 * movers, states, LANES))] * 2
            + [last(2, slots, wide_step), hbm],
            out_specs=[last(2, slots, wide_step), hbm],
            scratch_shapes=[
                pltpu.VMEM((grid, movers, states, wide_step), BF16),
                pltpu.VMEM((2, pad, wide_step), F32),
                pltpu.SemaphoreType.DMA((grid, movers)),
            ],
            input_output_aliases={1 + peers + 8: 1},
            compiler_params=params(32),
        )(land_tab, *[ssm_got[k] for k in range(1, n)], a_log, *moving, out_stay, new_ssm)
    return outputs, new_ssm, jnp.transpose(new_conv, (1, 0, 2))


def solution(mesh):
    return jax.shard_map(
        functools.partial(local, mesh.shape["inst"], mesh.shape["tp"]),
        mesh=mesh,
        in_specs=(
            P(None, ("groups", "inst"), "tp"),
            P(None, ("groups", "inst"), "tp"),
            P(("groups", "inst"), None, "tp"),
            P(("groups", "inst"), None, "tp"),
            P(None, "tp"),
            P("tp"),
            P("tp", None),
            P(None, "tp"),
            P("tp"),
            P(None, "tp"),
            P("tp"),
            P(("groups", "inst"), None),
            P("groups", None),
            P(("groups", "inst"), None),
        ),
        out_specs=(
            P(None, ("groups", "inst"), "tp"),
            P(("groups", "inst"), None, "tp"),
            P(("groups", "inst"), None, "tp"),
        ),
        check_vma=False,
    )
```

time: 145 us -> 90.7 us (0.63)
  local copies, waits for them, and re-layouts: 45.5 us -> 8.27 us
  Pallas kernels: 0 us -> 36.4 us
  other arithmetic: 24.5 us -> 0 us
  between operations: 14.4 us -> 0.77 us
  matrix products: 13.5 us -> 0 us
  waiting for transfers between devices: 37.3 us -> 31.5 us
  starting transfers between devices: 8.91 us -> 13.5 us
    psum x1 -> x0, waiting for transfers between devices: 37.3 us -> none  [local(): summed = lax.psum(partial_sum, 'tp')]
    pallas_call x0 -> x4, Pallas kernels: none -> 36.4 us  [the longest x1 18.6 us: local(): pl.pallas_call(functools.partial(stay_kernel, n, tps, cap, stays), grid=(...]
    ppermute x0 -> x9, waiting for transfers between devices: none -> 31.5 us  [exchange(): return lax.ppermute(value, axis, [(i, i ^ k) for i in range(n)])]
    scatter x6 -> x0, local copies, waits for them, and re-layouts: 24.2 us -> none  [the longest x1 6.68 us: local(): conv_state.at[flat_target]]
    reduce_sum x3 -> x0, other arithmetic: 16.1 us -> none  [the longest x1 14.7 us: local(): jnp.sum(c_part[:, :, None] * hidden, axis=1) + skip_gain * conv_out]
    ppermute x0 -> x9, starting transfers between devices: none -> 13.5 us  [exchange(): return lax.ppermute(value, axis, [(i, i ^ k) for i in range(n)])]
    dot_general x4 -> x0, matrix products: 13.5 us -> none  [the longest x2 7.44 us: local(): jnp.dot(conv_out.astype(jnp.bfloat16), proj_weight, preferred_element_typ...]
    all_to_all x2 -> x0, starting transfers between devices: 8.69 us -> none  [the longest x1 4.45 us: local(): lax.all_to_all(buf_ssm, 'inst', split_axis=0, concat_axis=0, tiled=True)]
  transfers between devices with their start and end apart: 3 -> 9, of which waited for: 1 -> 4; matrix products, arithmetic and copies ran while one was open for 34% -> 0% of each run, Pallas kernels for 0% -> 26%
where the time goes in v1:
time: 90.7 us; the launch traced here: 90.4 us
  Pallas kernels  36.4 us (40%)
  waiting for transfers between devices  31.5 us (35%)
  starting transfers between devices  13.5 us (15%)
  local copies, waits for them, and re-layouts  8.27 us (9%)
    ppermute x9, waiting for transfers between devices, exchange(): return lax.ppermute(value, axis, [(i, i ^ k) for i in range(n)])  31.5 us
    pallas_call x1, Pallas kernels, local(): pl.pallas_call(functools.partial(stay_kernel, n, tps, cap, stays), grid=(...  18.6 us
    ppermute x9, starting transfers between devices, exchange(): return lax.ppermute(value, axis, [(i, i ^ k) for i in range(n)])  13.5 us
    unnamed x32, local copies, waits for them, and re-layouts  8.27 us
    pallas_call x1, Pallas kernels, local(): pl.pallas_call(functools.partial(arrive_kernel, n, cap), grid=(grid,), ou...  6.86 us
    pallas_call x1, Pallas kernels, local(): pl.pallas_call(functools.partial(gather_kernel, n, cap, chunks), out_shap...  5.75 us
    pallas_call x1, Pallas kernels, local(): pl.pallas_call(functools.partial(project_kernel, n, cap), grid=(chunks,),...  5.26 us
  transfers between devices with their start and end apart: 9, of which 4 were waited for; matrix products, arithmetic and copies ran while one was open for 0% of the time, Pallas kernels for 26%

profile of v1, /device:TPU:0, one launch (start us, length us, event | category | flops | bytes accessed | tf_op | source)
XLA Modules:
  0.0 90.4 jit_solution(5459891552005407285)
XLA Ops:
  0.7 2.8 %copy-done = bf16[48,16,4096]{2,1,0:T(8,128)(2,1)S(1)} copy-done((bf16[48,16,4096]{2,1,0:T(8,128)(2,1)S(1)}, bf16[48,16,4096]{2,1,0:T(8,128)(2,1)}, u32[]{:S(2)}) %copy-start) | copy-done | bytes 6291480
  3.4 1.3 %copy-done.2 = bf16[48,3,4096]{2,0,1:T(8,128)(2,1)S(1)} copy-done((bf16[48,3,4096]{2,0,1:T(8,128)(2,1)S(1)}, bf16[48,3,4096]{2,0,1:T(8,128)(2,1)}, u32[]{:S(2)}) %copy-start.2) | copy-done | bytes 1179672
  4.7 0.7 copy-done.13
  5.4 0.7 copy-done.14
  6.0 0.7 copy-done.15
  6.7 5.7 %gather_leaving.1 = (bf16[48,1024]{1,0:T(8,128)(2,1)S(1)}, bf16[48,1024]{1,0:T(8,128)(2,1)S(1)}, bf16[48,1024]{1,0:T(8,128)(2,1)S(1)}, bf16[4,16,4096]{2,1,0:T(8...) custom-call(s32[1,12]{1,0:T(1,128)S(1)} %copy-done.14, ...), custom_call_target="tpu_custom_call" | custom-call | tf_op jit(solution)/shard_map/gather_leaving/pallas_call | solution.py:410
  12.5 0.0 copy-start.6
  12.5 0.5 collective-permute-start
  13.0 2.6 %collective-permute-start.1 = (bf16[4,16,4096]{2,1,0:T(8,128)(2,1)S(1)}, bf16[4,16,4096]{2,1,0:T(8,128)(2,1)S(1)}, u32[]{:S(2)}, u32[]{:S(2)}) collective-permute-start(bf16[4,16,4096]{2,1,0:T(8,128)(2,1)S(1)} %get-tuple-element.27), channel_id=1, source_target_pairs={{0,8},{4,12},{8,0},{12,4},{1,9},{5,13},{9,1},{13,5},{2,10},{6,14},... | collective-permute-start | bytes 1572872 | tf_op jit(solution)/shard_map/ppermute | solution.py:350
  15.6 0.1 collective-permute-start.2
  15.7 0.1 collective-permute-start.3
  15.8 1.9 %collective-permute-start.4 = (bf16[48,1024]{1,0:T(8,128)(2,1)S(1)}, bf16[48,1024]{1,0:T(8,128)(2,1)S(1)}, u32[]{:S(2)}, u32[]{:S(2)}) collective-permute-start(bf16[48,1024]{1,0:T(8,128)(2,1)S(1)} %get-tuple-element.31), channel_id=1, source_target_pairs={{0,8},{4,12},{8,0},{12,4},{1,9},{5,13},{9,1},{13,5},{2,10},{6,14},... | collective-permute-start | bytes 294920 | tf_op jit(solution)/shard_map/ppermute | solution.py:350
  17.8 0.9 collective-permute-start.5
  18.7 23.1 %collective-permute-done.4.rest_1_ = bf16[48,1024]{1,0:T(8,128)(2,1)S(1)} collective-permute-done((bf16[48,1024]{1,0:T(8,128)(2,1)S(1)}, bf16[48,1024]{1,0:T(8,128)(2,1)S(1)}, u32[]{:S(2)}, u32[]{:S(2)}) %collective-permute-start.4) | collective-permute-done | bytes 98336 | tf_op jit(solution)/shard_map/ppermute | solution.py:350
  41.8 1.6 %collective-permute-done.5.rest_2_ = bf16[48,1024]{1,0:T(8,128)(2,1)S(1)} collective-permute-done((bf16[48,1024]{1,0:T(8,128)(2,1)S(1)}, bf16[48,1024]{1,0:T(8,128)(2,1)S(1)}, u32[]{:S(2)}, u32[]{:S(2)}) %collective-permute-start.5) | collective-permute-done | bytes 98336 | tf_op jit(solution)/shard_map/ppermute | solution.py:350
  43.4 5.3 %project.1 = (f32[2,48,4096]{2,1,0:T(8,128)S(1)}, bf16[3,48,4096]{2,1,0:T(8,128)(2,1)}, f32[96,640]{1,0:T(8,128)S(1)}, bf16[96,640]{1,0:T(8,128)(2,1)S(1)}) custom-call(s32[16]{0:T(128)S(1)} %get-tuple-element.25.land_tab, bf16[48,1024]{1,0:T(8,128)(2,1)S(1)} %collective-permute-done.3.rest_0_, bf16[48,1024]{1,0:T(8,128)(2,1)S(1)} %collective-permute-done.4.rest_1_, ...), custom_call_target="tpu_custom_call" | custom-call | tf_op jit(solution)/shard_map/project/pallas_call | solution.py:435
  48.6 1.6 %collective-permute-start.8 = (bf16[96,640]{1,0:T(8,128)(2,1)S(1)}, bf16[96,640]{1,0:T(8,128)(2,1)S(1)}, u32[]{:S(2)}, u32[]{:S(2)}) collective-permute-start(bf16[96,640]{1,0:T(8,128)(2,1)S(1)} %get-tuple-element.34), channel_id=1, source_target_pairs={{0,1},{1,0},{2,3},{3,2},{4,5},{5,4},{6,7},{7,6},{8,9},{9,8},{10,11... | collective-permute-start | bytes 368648 | tf_op jit(solution)/shard_map/ppermute | solution.py:350
  50.3 2.6 %collective-permute-start.7 = (bf16[96,640]{1,0:T(8,128)(2,1)S(1)}, bf16[96,640]{1,0:T(8,128)(2,1)S(1)}, u32[]{:S(2)}, u32[]{:S(2)}) collective-permute-start(bf16[96,640]{1,0:T(8,128)(2,1)S(1)} %get-tuple-element.34), channel_id=1, source_target_pairs={{0,2},{1,3},{2,0},{3,1},{4,6},{5,7},{6,4},{7,5},{8,10},{9,11},{10,... | collective-permute-start | bytes 368648 | tf_op jit(solution)/shard_map/ppermute | solution.py:350
  52.8 3.2 %collective-permute-done.8.rest_2_ = bf16[96,640]{1,0:T(8,128)(2,1)S(1)} collective-permute-done((bf16[96,640]{1,0:T(8,128)(2,1)S(1)}, bf16[96,640]{1,0:T(8,128)(2,1)S(1)}, u32[]{:S(2)}, u32[]{:S(2)}) %collective-permute-start.8) | collective-permute-done | bytes 122912 | tf_op jit(solution)/shard_map/ppermute | solution.py:350
  56.0 3.2 %collective-permute-start.6 = (bf16[96,640]{1,0:T(8,128)(2,1)S(1)}, bf16[96,640]{1,0:T(8,128)(2,1)S(1)}, u32[]{:S(2)}, u32[]{:S(2)}) collective-permute-start(bf16[96,640]{1,0:T(8,128)(2,1)S(1)} %get-tuple-element.34), channel_id=1, source_target_pairs={{0,3},{1,2},{2,1},{3,0},{4,7},{5,6},{6,5},{7,4},{8,11},{9,10},{10,... | collective-permute-start | bytes 368648 | tf_op jit(solution)/shard_map/ppermute | solution.py:350
  59.2 3.6 %collective-permute-done.6.rest_0_ = bf16[96,640]{1,0:T(8,128)(2,1)S(1)} collective-permute-done((bf16[96,640]{1,0:T(8,128)(2,1)S(1)}, bf16[96,640]{1,0:T(8,128)(2,1)S(1)}, u32[]{:S(2)}, u32[]{:S(2)}) %collective-permute-start.6) | collective-permute-done | bytes 122912 | tf_op jit(solution)/shard_map/ppermute | solution.py:350
  62.8 2.2 %copy-done.5 = bf16[512,4096]{1,0:T(8,128)(2,1)S(1)} copy-done((bf16[512,4096]{1,0:T(8,128)(2,1)S(1)}, bf16[512,4096]{1,0:T(8,128)(2,1)}, u32[]{:S(2)}) %copy-start.5) | copy-done | bytes 4194328
  65.0 18.6 %update_staying.1 = (bf16[48,16,4096]{2,1,0:T(8,128)(2,1)}, bf16[2,48,4096]{2,1,0:T(8,128)(2,1)S(1)}, f32[24,4096]{1,0:T(8,128)S(1)}, f32[24,4096]{1,0:T(8,128)S...) custom-call(s32[16]{0:T(128)S(1)} %get-tuple-element.25.land_tab, ...), custom_call_target="tpu_custom_call" | custom-call | tf_op jit(solution)/shard_map/update_staying/pallas_call | solution.py:475
  83.6 6.9 %update_arrived.1 = (bf16[2,48,4096]{2,1,0:T(8,128)(2,1)}, bf16[48,16,4096]{2,1,0:T(8,128)(2,1)}) custom-call(s32[16]{0:T(128)S(1)} %get-tuple-element.25.land_tab, bf16[4,16,4096]{2,1,0:T(8,128)(2,1)S(1)} %collective-permute-done.rest_0_, bf16[4,16,4096]{2,1,0:T(8,128)(2,1)S(1)} %collective-permute-done.1.rest_1_, ...), custom_call_target="tpu_custom_call", output_to_operand_aliasing={{1}: (12, {})} | custom-call | tf_op jit(solution)/shard_map/update_arrived/pallas_call | solution.py:528
  (30 shorter events, 0.1 us)
Async XLA Ops:
  0.6 2.8 %copy-start = (bf16[48,16,4096]{2,1,0:T(8,128)(2,1)S(1)}, bf16[48,16,4096]{2,1,0:T(8,128)(2,1)}, u32[]{:S(2)}) copy-start(bf16[48,16,4096]{2,1,0:T(8,128)(2,1)} %rest_9_.1) | copy-start | bytes 18874372
  3.4 1.3 %copy-start.2 = (bf16[48,3,4096]{2,0,1:T(8,128)(2,1)S(1)}, bf16[48,3,4096]{2,0,1:T(8,128)(2,1)}, u32[]{:S(2)}) copy-start(bf16[48,3,4096]{2,0,1:T(8,128)(2,1)} %param.17) | copy-start | bytes 3538948
  4.7 0.7 copy-start.13
  5.4 0.7 copy-start.14
  6.7 36.7 %copy-start.3 = (bf16[48,3,4096]{2,0,1:T(8,128)(2,1)S(1)}, bf16[48,3,4096]{2,0,1:T(8,128)(2,1)}, u32[]{:S(2)}) copy-start(bf16[48,3,4096]{2,0,1:T(8,128)(2,1)} %param.17) | copy-start | bytes 3538948
  6.7 36.7 %copy-start.4 = (bf16[4096,544]{0,1:T(8,128)(2,1)S(1)}, bf16[4096,544]{0,1:T(8,128)(2,1)}, u32[]{:S(2)}) copy-start(bf16[4096,544]{0,1:T(8,128)(2,1)} %param.20) | copy-start | bytes 13369348
  6.7 36.7 %copy-start.8 = (bf16[2,48,4096]{2,1,0:T(8,128)(2,1)S(1)}, bf16[2,48,4096]{2,1,0:T(8,128)(2,1)}, u32[]{:S(2)}) copy-start(bf16[2,48,4096]{2,1,0:T(8,128)(2,1)} %rest_4_.1) | copy-start | bytes 2359300
  6.7 36.7 %copy-start.9 = (f32[4,4096]{1,0:T(4,128)S(1)}, f32[4,4096]{1,0:T(4,128)}, u32[]{:S(2)}) copy-start(f32[4,4096]{1,0:T(4,128)} %rest_5_.2) | copy-start | bytes 196612
  6.7 36.7 %copy-start.10 = (f32[4096]{0:T(1024)S(1)}, f32[4096]{0:T(1024)}, u32[]{:S(2)}) copy-start(f32[4096]{0:T(1024)} %param.19) | copy-start | bytes 49156
  6.7 56.1 %copy-start.7 = (bf16[2,48,4096]{2,1,0:T(8,128)(2,1)S(1)}, bf16[2,48,4096]{2,1,0:T(8,128)(2,1)}, u32[]{:S(2)}) copy-start(bf16[2,48,4096]{2,1,0:T(8,128)(2,1)} %rest_8_.1) | copy-start | bytes 2359300
  12.5 50.3 %copy-start.1 = (bf16[48,16,4096]{2,1,0:T(8,128)(2,1)S(1)}, bf16[48,16,4096]{2,1,0:T(8,128)(2,1)}, u32[]{:S(2)}) copy-start(bf16[48,16,4096]{2,1,0:T(8,128)(2,1)} %rest_9_.1) | copy-start | bytes 18874372
  12.5 50.3 %copy-start.6 = (f32[16,4096]{1,0:T(8,128)S(1)}, f32[16,4096]{1,0:T(8,128)}, u32[]{:S(2)}) copy-start(f32[16,4096]{1,0:T(8,128)} %rest_3_.3) | copy-start | bytes 786436
  12.5 50.3 %copy-start.11 = (f32[4096]{0:T(1024)S(1)}, f32[4096]{0:T(1024)}, u32[]{:S(2)}) copy-start(f32[4096]{0:T(1024)} %param.22) | copy-start | bytes 49156
  12.5 50.3 %copy-start.12 = (f32[4096]{0:T(1024)S(1)}, f32[4096]{0:T(1024)}, u32[]{:S(2)}) copy-start(f32[4096]{0:T(1024)} %param.24) | copy-start | bytes 49156
  12.5 71.0 %collective-permute-start = (bf16[4,16,4096]{2,1,0:T(8,128)(2,1)S(1)}, bf16[4,16,4096]{2,1,0:T(8,128)(2,1)S(1)}, u32[]{:S(2)}, u32[]{:S(2)}) collective-permute-start(bf16[4,16,4096]{2,1,0:T(8,128)(2,1)S(1)} %get-tuple-element.26), channel_id=1, source_target_pairs={{0,4},{4,0},{8,12},{12,8},{1,5},{5,1},{9,13},{13,9},{2,6},{6,2},{1... | collective-permute-start | bytes 1572872 | tf_op jit(solution)/shard_map/ppermute | solution.py:350
  13.0 70.5 %collective-permute-start.1 = (bf16[4,16,4096]{2,1,0:T(8,128)(2,1)S(1)}, bf16[4,16,4096]{2,1,0:T(8,128)(2,1)S(1)}, u32[]{:S(2)}, u32[]{:S(2)}) collective-permute-start(bf16[4,16,4096]{2,1,0:T(8,128)(2,1)S(1)} %get-tuple-element.27), channel_id=1, source_target_pairs={{0,8},{4,12},{8,0},{12,4},{1,9},{5,13},{9,1},{13,5},{2,10},{6,14},... | collective-permute-start | bytes 1572872 | tf_op jit(solution)/shard_map/ppermute | solution.py:350
  15.6 67.9 %collective-permute-start.2 = (bf16[4,16,4096]{2,1,0:T(8,128)(2,1)S(1)}, bf16[4,16,4096]{2,1,0:T(8,128)(2,1)S(1)}, u32[]{:S(2)}, u32[]{:S(2)}) collective-permute-start(bf16[4,16,4096]{2,1,0:T(8,128)(2,1)S(1)} %get-tuple-element.28), channel_id=1, source_target_pairs={{0,12},{4,8},{8,4},{12,0},{1,13},{5,9},{9,5},{13,1},{2,14},{6,10},... | collective-permute-start | bytes 1572872 | tf_op jit(solution)/shard_map/ppermute | solution.py:350
  15.7 2.1 %collective-permute-start.3 = (bf16[48,1024]{1,0:T(8,128)(2,1)S(1)}, bf16[48,1024]{1,0:T(8,128)(2,1)S(1)}, u32[]{:S(2)}, u32[]{:S(2)}) collective-permute-start(bf16[48,1024]{1,0:T(8,128)(2,1)S(1)} %get-tuple-element.30), channel_id=1, source_target_pairs={{0,4},{4,0},{8,12},{12,8},{1,5},{5,1},{9,13},{13,9},{2,6},{6,2},{1... | collective-permute-start | bytes 294920 | tf_op jit(solution)/shard_map/ppermute | solution.py:350
  15.8 25.9 %collective-permute-start.4 = (bf16[48,1024]{1,0:T(8,128)(2,1)S(1)}, bf16[48,1024]{1,0:T(8,128)(2,1)S(1)}, u32[]{:S(2)}, u32[]{:S(2)}) collective-permute-start(bf16[48,1024]{1,0:T(8,128)(2,1)S(1)} %get-tuple-element.31), channel_id=1, source_target_pairs={{0,8},{4,12},{8,0},{12,4},{1,9},{5,13},{9,1},{13,5},{2,10},{6,14},... | collective-permute-start | bytes 294920 | tf_op jit(solution)/shard_map/ppermute | solution.py:350
  17.8 25.6 %collective-permute-start.5 = (bf16[48,1024]{1,0:T(8,128)(2,1)S(1)}, bf16[48,1024]{1,0:T(8,128)(2,1)S(1)}, u32[]{:S(2)}, u32[]{:S(2)}) collective-permute-start(bf16[48,1024]{1,0:T(8,128)(2,1)S(1)} %get-tuple-element.32), channel_id=1, source_target_pairs={{0,12},{4,8},{8,4},{12,0},{1,13},{5,9},{9,5},{13,1},{2,14},{6,10},... | collective-permute-start | bytes 294920 | tf_op jit(solution)/shard_map/ppermute | solution.py:350
  48.6 7.4 %collective-permute-start.8 = (bf16[96,640]{1,0:T(8,128)(2,1)S(1)}, bf16[96,640]{1,0:T(8,128)(2,1)S(1)}, u32[]{:S(2)}, u32[]{:S(2)}) collective-permute-start(bf16[96,640]{1,0:T(8,128)(2,1)S(1)} %get-tuple-element.34), channel_id=1, source_target_pairs={{0,1},{1,0},{2,3},{3,2},{4,5},{5,4},{6,7},{7,6},{8,9},{9,8},{10,11... | collective-permute-start | bytes 368648 | tf_op jit(solution)/shard_map/ppermute | solution.py:350
  50.3 8.9 %collective-permute-start.7 = (bf16[96,640]{1,0:T(8,128)(2,1)S(1)}, bf16[96,640]{1,0:T(8,128)(2,1)S(1)}, u32[]{:S(2)}, u32[]{:S(2)}) collective-permute-start(bf16[96,640]{1,0:T(8,128)(2,1)S(1)} %get-tuple-element.34), channel_id=1, source_target_pairs={{0,2},{1,3},{2,0},{3,1},{4,6},{5,7},{6,4},{7,5},{8,10},{9,11},{10,... | collective-permute-start | bytes 368648 | tf_op jit(solution)/shard_map/ppermute | solution.py:350
  56.0 6.8 %collective-permute-start.6 = (bf16[96,640]{1,0:T(8,128)(2,1)S(1)}, bf16[96,640]{1,0:T(8,128)(2,1)S(1)}, u32[]{:S(2)}, u32[]{:S(2)}) collective-permute-start(bf16[96,640]{1,0:T(8,128)(2,1)S(1)} %get-tuple-element.34), channel_id=1, source_target_pairs={{0,3},{1,2},{2,1},{3,0},{4,7},{5,6},{6,5},{7,4},{8,11},{9,10},{10,... | collective-permute-start | bytes 368648 | tf_op jit(solution)/shard_map/ppermute | solution.py:350
  62.8 2.2 %copy-start.5 = (bf16[512,4096]{1,0:T(8,128)(2,1)S(1)}, bf16[512,4096]{1,0:T(8,128)(2,1)}, u32[]{:S(2)}) copy-start(bf16[512,4096]{1,0:T(8,128)(2,1)} %rest_3_.2) | copy-start | bytes 12582916
  (1 other events, 0.7 us)

commit v2 on v0

v2 whole, which is shorter than its diff:
```python
import functools
import math

import jax
import jax.numpy as jnp
from jax import lax
from jax.experimental import pallas as pl
from jax.experimental.pallas import tpu as pltpu
from jax.sharding import PartitionSpec as P

F32 = jnp.float32
BF16 = jnp.bfloat16
LANES = 128
LOG2E = math.log2(math.e)
MIB = 1 << 20


def iota(shape, dim):
    return lax.broadcasted_iota(jnp.int32, shape, dim)


def silu(value):
    return value / (1.0 + jnp.exp(-value))


def gather_conv_kernel(n, cap, chunks, own_ref, leave_hbm, dest_hbm, conv_hbm, ssm, *rest):
    peers = n - 1
    send = rest[:peers]
    near, leave_tab, leave, dest, conv, sems, row_sems = rest[peers:]
    mig = leave.shape[1]
    taps, slots, channels = conv.shape
    width = channels // chunks
    own = own_ref[0]
    tables = [
        pltpu.make_async_copy(leave_hbm, leave, sems.at[chunks]),
        pltpu.make_async_copy(dest_hbm, dest, sems.at[chunks + 1]),
    ]
    for table in tables:
        table.start()
    loads = []
    for q in range(chunks):
        lanes = pl.ds(q * width, width)
        loads.append(pltpu.make_async_copy(conv_hbm.at[:, :, lanes], conv.at[:, :, lanes], sems.at[q]))
        loads[q].start()
    for i in range(n * cap):
        leave_tab[i] = -1
    for table in tables:
        table.wait()
    away = [dest[own, pos] ^ own for pos in range(mig)]
    for pos in range(mig):
        place = 0
        for earlier in range(pos):
            place = place + jnp.where(away[earlier] == away[pos], 1, 0)
        leave_tab[away[pos] * cap + place] = leave[0, pos]
    pairs = row_copies(ssm, [near], row_sems, leave_tab, cap, [1])
    start_all(pairs)

    rows = chunks * taps * cap
    row = iota((peers * rows, 1), 0)
    inner = lax.rem(row, rows)
    place = lax.rem(inner, cap)
    tap = lax.rem(lax.div(inner, cap), taps)
    chunk = lax.div(inner, taps * cap)
    peer = lax.div(row, rows)
    source = jnp.full(row.shape, -1, jnp.int32)
    for k in range(1, n):
        for s in range(cap):
            slot = leave_tab[k * cap + s]
            source = jnp.where((peer == k - 1) & (place == s) & (slot >= 0), tap * slots + slot, source)
    pick = jnp.where(source == iota((peers * rows, taps * slots), 1), 1.0, 0.0)
    total = None
    for q in range(chunks):
        loads[q].wait()
        part = jnp.dot(
            jnp.where(chunk == q, pick, 0.0).astype(BF16),
            conv[:, :, q * width : (q + 1) * width].reshape(taps * slots, width),
            preferred_element_type=F32,
        )
        total = part if total is None else total + part
    for k in range(1, n):
        send[k - 1][...] = total[(k - 1) * rows : k * rows, :].astype(BF16)
    wait_all(pairs)


def row_copies(ssm, send, sems, tab, cap, peer_list):
    pairs = []
    for at, k in enumerate(peer_list):
        for s in range(cap):
            slot = tab[k * cap + s]
            pairs.append((slot >= 0, pltpu.make_async_copy(ssm.at[slot], send[at].at[s], sems.at[at, s])))
    return pairs


def start_all(pairs):
    for present, copy in pairs:
        pl.when(present)(copy.start)


def wait_all(pairs):
    for present, copy in pairs:
        pl.when(present)(copy.wait)


def gather_ssm_kernel(n, cap, peer_list, own_ref, leave_tab, leave_hbm, dest_hbm, land_hbm, ssm, _, *rest):
    send = rest[: len(peer_list)]
    land_tab, stay_tab, leave, dest, land, flags, sems, table_sems = rest[len(peer_list) :]
    mig = leave.shape[1]
    slots = ssm.shape[0]
    own = own_ref[0]
    tables = [
        pltpu.make_async_copy(source, target, table_sems.at[i])
        for i, (source, target) in enumerate(((leave_hbm, leave), (dest_hbm, dest), (land_hbm, land)))
    ]
    for table in tables:
        table.start()
    pairs = row_copies(ssm, send, sems, leave_tab, cap, peer_list)
    start_all(pairs)
    for i in range(n * cap + 1):
        land_tab[i] = -1
    for i in range(slots):
        flags[i] = 0
    for table in tables:
        table.wait()

    def arrivals(source, rank):
        base = (source ^ own) * cap
        place = 0
        for pos in range(mig):
            hit = jnp.where(dest[source, pos] == own, 1, 0)
            land_tab[jnp.where(hit == 1, base + place, n * cap)] = land[0, jnp.minimum(rank, mig - 1)]
            rank, place = rank + hit, place + hit
        return rank

    if n <= 4:
        rank = 0
        for source in range(n):
            rank = arrivals(source, rank)
    else:
        lax.fori_loop(0, n, arrivals, 0)
    for pos in range(mig):
        flags[leave[0, pos]] = 1
    count = 0
    for slot in range(slots):
        stay_tab[count] = slot
        count = count + 1 - flags[slot]
    wait_all(pairs)


def project_kernel(n, cap, chunks, land_tab, _, *rest):
    peers = n - 1
    got = rest[:peers]
    conv, x_new, weight, bias, proj = rest[peers : peers + 5]
    conv_out, new_conv, own_sum, send_sum, newest, sems = rest[peers + 5 :]
    taps, slots, channels = conv.shape
    width = channels // chunks
    rows = got[0].shape[0]
    cols = proj.shape[0]
    store = [pltpu.make_async_copy(x_new.at[t], new_conv.at[taps - 2 + t], sems.at[t]) for t in range(2)]
    store.append(pltpu.make_async_copy(newest, new_conv.at[0], sems.at[2]))
    store[0].start()
    store[1].start()

    col = iota((1, peers * rows), 1)
    inner = lax.rem(col, rows)
    target = jnp.full(col.shape, -1, jnp.int32)
    slot_row = iota((slots, 1), 0)
    arrived = jnp.zeros((slots, 1), jnp.bool_)
    for k in range(1, n):
        for s in range(cap):
            slot = land_tab[k * cap + s]
            target = jnp.where((lax.div(col, rows) == k - 1) & (lax.rem(inner, cap) == s), slot, target)
            arrived = arrived | (slot_row == slot)
    tap = lax.rem(lax.div(inner, cap), taps)
    chunk = lax.div(inner, taps * cap)
    grid_row = iota((slots, peers * rows), 0)
    incoming = jnp.concatenate([g[...] for g in got], axis=0)
    total = jnp.zeros((2 * slots, cols), F32)
    for q in range(chunks):
        lanes = slice(q * width, (q + 1) * width)
        history = []
        for j in range(taps):
            pick = grid_row == jnp.where((tap == j) & (chunk == q), target, -1)
            moved = jnp.dot(jnp.where(pick, 1.0, 0.0).astype(BF16), incoming, preferred_element_type=F32)
            history.append(jnp.where(arrived, moved, conv[j, :, lanes].astype(F32)))
        newest[:, lanes] = history[taps - 1].astype(BF16)
        window = history + [x_new[t, :, lanes].astype(F32) for t in range(2)]
        halves = []
        for t in range(2):
            value = window[t] * weight[0:1, lanes]
            for j in range(1, taps + 1):
                value += window[t + j] * weight[j : j + 1, lanes]
            value = silu(value + bias[:, lanes])
            conv_out[t * slots : (t + 1) * slots, lanes] = value
            halves.append(value.astype(BF16))
        total += lax.dot_general(
            jnp.concatenate(halves, axis=0),
            proj[:, lanes],
            (((1,), (1,)), ((), ())),
            preferred_element_type=F32,
        )
    store[2].start()
    padded = own_sum.shape[1]
    rank = padded - LANES
    own_sum[:, rank:] = jnp.zeros((2 * slots, LANES), F32)
    own_sum[:, :cols] = total
    tail = own_sum[:, rank:]
    send_sum[:, :rank] = total[:, :rank].astype(BF16)
    high = tail.astype(BF16).astype(F32)
    send_sum[:, rank:] = (high + pltpu.roll(tail - high, cols - rank, 1)).astype(BF16)
    for copy in store:
        copy.wait()


def spread(values, lane, states):
    rows = values.shape[0]
    wide = jnp.broadcast_to(values[:, None, :], (rows, states, LANES))
    keep = iota(wide.shape, 2) == iota(wide.shape, 1) + lane
    wide = jnp.where(keep, wide, 0.0).reshape(rows * states, LANES)
    high = wide.astype(BF16)
    low = (wide - high.astype(F32)).astype(BF16)
    ones = jnp.ones((LANES, LANES), BF16)
    both = jnp.dot(high, ones, preferred_element_type=F32) + jnp.dot(low, ones, preferred_element_type=F32)
    return both.reshape(rows, states, LANES)


def spread_diagonal(values, lane, states, rows):
    cols = rows * states
    pick = iota((LANES, cols), 0) == lax.rem(iota((LANES, cols), 1), states) + lane
    pick = jnp.where(pick, 1.0, 0.0).astype(BF16)
    keep = lax.div(iota((values.shape[0], cols), 1), states) == iota((values.shape[0], cols), 0)
    high = values.astype(BF16)
    low = (values - high.astype(F32)).astype(BF16)
    parts = [jnp.where(keep, jnp.dot(v, pick, preferred_element_type=F32), 0.0) for v in (high, low)]
    return jnp.concatenate(parts, axis=0).astype(BF16)


def read(weights, hidden):
    both = jnp.dot(weights, hidden.reshape(-1, hidden.shape[2]), preferred_element_type=F32)
    half = both.shape[0] // 2
    return both[:half] + both[half:]


def advance(hidden, rate, size, drive, b_part):
    return jnp.exp2(size * rate) * hidden + drive * b_part


def wide(tile, lanes):
    return jnp.concatenate([tile] * (lanes // LANES), axis=1)


def gate_kernel(n, cap, land_tab, conv_out, z_new, skip, a_log, ssm, dt_weight, *rest):
    ssm_held, weight_held, gate, skipped, rate, conv_m, skip_m, gate_m, sems = rest
    slots = conv_out.shape[0] // 2
    held = [
        pltpu.make_async_copy(ssm, ssm_held, sems.at[0]),
        pltpu.make_async_copy(dt_weight, weight_held, sems.at[1]),
    ]
    for copy in held:
        copy.start()
    gate[...] = silu(z_new[...].astype(F32))
    skipped[...] = skip[...] * conv_out[...]
    rate[...] = -LOG2E * jnp.exp(a_log[...])
    movers = (n - 1) * cap
    for t in range(2):
        for i in range(movers):
            from_row = pl.ds(t * slots + jnp.maximum(land_tab[cap + i], 0), 1)
            at = t * movers + i
            for ref, source in ((conv_m, conv_out), (skip_m, skipped), (gate_m, gate)):
                ref[at : at + 1, :] = source[from_row, :]
    for copy in held:
        copy.wait()


def stay_kernel(n, tps, cap, stays, step, land_tab, stay_tab, own_sum, *rest):
    got = rest[: tps - 1]
    dt_weight, dt_bias, rate_ref, conv_out, skipped, gate, conv_m, ssm = rest[tps - 1 : tps + 7]
    new_ssm, out, size_m, drive_m, b_m, c_m = rest[tps + 7 : tps + 13]
    b_all, c_all, size_s, drive_s, middle, fresh, sems = rest[tps + 13 :]
    rank = dt_weight.shape[0]
    states, channels = rate_ref.shape
    slots = ssm.shape[0]
    movers = (n - 1) * cap

    raw = own_sum[:, :rank]
    tail = own_sum[:, rank:]
    for g in got:
        raw += g[:, :rank].astype(F32)
        piece = g[:, rank:].astype(F32)
        tail += piece + pltpu.roll(piece, LANES - 2 * states, 1)
    scale = lax.rsqrt(jnp.mean(raw * raw, axis=1, keepdims=True) + 1e-06)
    normed = (raw * scale).astype(BF16)
    b_all[...] = spread(tail, 0, states)
    middle[...] = jnp.zeros_like(middle)
    pad = c_m.shape[1] // 2
    row = iota((pad, slots), 0)
    slot_of = jnp.full(row.shape, -1, jnp.int32)
    for i in range(movers):
        slot_of = jnp.where(row == i, land_tab[cap + i], slot_of)
    pick = jnp.where(slot_of == iota((pad, slots), 1), 1.0, 0.0)
    for t in range(2):
        mine = tail[t * slots : (t + 1) * slots]
        c_all[t] = spread_diagonal(mine, states, states, slots)
        moved = jnp.dot(pick, mine, preferred_element_type=F32, precision=lax.Precision.HIGHEST)
        c_m[t] = spread_diagonal(moved, states, states, movers)
        for i in range(movers):
            b_m[t * movers + i] = b_all[t * slots + jnp.maximum(land_tab[cap + i], 0)]

    def store(place, lanes):
        return pltpu.make_async_copy(fresh.at[place], new_ssm.at[:, :, lanes], sems.at[place])

    def chunk(place, _):
        lanes = pl.ds(pl.multiple_of(place * step, step), step)
        pre = jnp.dot(normed, dt_weight[:, lanes], preferred_element_type=F32) + dt_bias[:, lanes]
        size = jnp.maximum(pre, 0.0) + jnp.log1p(jnp.exp(-jnp.abs(pre)))
        size_s[...] = size
        drive_s[...] = size * conv_out[:, lanes]
        rate = rate_ref[:, lanes]

        for i in range(movers):
            fresh[place, jnp.maximum(land_tab[cap + i], 0)] = jnp.zeros((states, step), BF16)

        def one(i, _):
            slot = stay_tab[i]
            hidden = ssm[slot, :, lanes].astype(F32)
            for t, after in ((0, middle.at[slot]), (1, fresh.at[place, slot])):
                at = pl.ds(t * slots + slot, 1)
                hidden = advance(hidden, rate, size_s[at, :], drive_s[at, :], wide(b_all[t * slots + slot], step))
                after[...] = hidden.astype(BF16)
            return 0

        lax.fori_loop(0, stays, one, 0, unroll=4)
        store(place, lanes).start()
        for t, after in ((0, middle[...]), (1, fresh[place])):
            at = slice(t * slots, (t + 1) * slots)
            out[at, lanes] = ((read(c_all[t], after) + skipped[at, lanes]) * gate[at, lanes]).astype(BF16)
        for t in range(2):
            for i in range(movers):
                from_row = pl.ds(t * slots + jnp.maximum(land_tab[cap + i], 0), 1)
                at = t * movers + i
                here = size_s[from_row, :]
                size_m[at : at + 1, lanes] = here
                drive_m[at : at + 1, lanes] = here * conv_m[at : at + 1, lanes]
        return 0

    lax.fori_loop(0, channels // step, chunk, 0)
    for place in range(channels // step):
        store(place, pl.ds(place * step, step)).wait()


def arrive_kernel(n, cap, full, step, land_tab, *rest):
    peers = n - 1
    got = rest[:peers]
    rate_ref, size_m, drive_m, skip_m, gate_m, b_m, c_m, out_in, _ = rest[peers : peers + 9]
    out, new_ssm, middle, fresh, rows_s, done_s, sems, out_sems = rest[peers + 9 :]
    states, channels = rate_ref.shape
    movers = peers * cap
    slots = out.shape[1]
    pad = rows_s.shape[1]
    row = iota((slots, pad), 0)
    col = iota((1, pad), 1)
    target = jnp.full(col.shape, -1, jnp.int32)
    arrived = jnp.zeros((slots, 1), jnp.bool_)
    slot_row = iota((slots, 1), 0)
    for i in range(movers):
        slot = land_tab[cap + i]
        target = jnp.where(col == i, slot, target)
        arrived = arrived | (slot_row == slot)
    pick = jnp.where(row == target, 1.0, 0.0).astype(BF16)
    rows_s[...] = jnp.zeros_like(rows_s)

    def copy(i, lanes, place):
        return pltpu.make_async_copy(fresh.at[place, i], new_ssm.at[land_tab[cap + i], :, lanes], sems.at[place, i])

    def copy_out(lanes, place):
        return pltpu.make_async_copy(done_s.at[place], out.at[:, :, lanes], out_sems.at[place])

    def chunk(place, _):
        lanes = pl.ds(pl.multiple_of(place * step, step), step)
        rate = rate_ref[:, lanes]
        for i in range(movers):
            hidden = got[i // cap][i % cap, :, lanes].astype(F32)
            if movers != full:
                hidden = jnp.where(land_tab[cap + i] >= 0, hidden, 0.0)
            for t, after in ((0, middle.at[i]), (1, fresh.at[place, i])):
                at = slice(t * movers + i, t * movers + i + 1)
                hidden = advance(hidden, rate, size_m[at, lanes], drive_m[at, lanes], wide(b_m[t * movers + i], step))
                after[...] = hidden.astype(BF16)
        for i in range(movers):
            pl.when(land_tab[cap + i] >= 0)(copy(i, lanes, place).start)
        for t in range(2):
            after = middle[...] if t == 0 else fresh[place]
            at = slice(t * movers, (t + 1) * movers)
            rows_s[t, :movers, :] = (read(c_m[t], after)[:movers] + skip_m[at, lanes]) * gate_m[at, lanes]
            placed = jnp.dot(pick, rows_s[t].astype(BF16), preferred_element_type=F32)
            kept = out_in[t * slots : (t + 1) * slots, lanes].astype(F32)
            done_s[place, t] = jnp.where(arrived, placed, kept).astype(BF16)
        copy_out(lanes, place).start()
        return 0

    lax.fori_loop(0, channels // step, chunk, 0)
    for place in range(channels // step):
        lanes = pl.ds(place * step, step)
        copy_out(lanes, place).wait()
        for i in range(movers):
            pl.when(land_tab[cap + i] >= 0)(copy(i, lanes, place).wait)


def exchange(value, axis, k, n):
    return lax.ppermute(value, axis, [(i, i ^ k) for i in range(n)])


def cost(flops):
    return pl.CostEstimate(flops=flops, bytes_accessed=0, transcendentals=0)


def params(mib):
    return pltpu.CompilerParams(vmem_limit_bytes=mib * MIB)


def local(
    n,
    tps,
    x_new,
    z_new,
    ssm_state,
    conv_state,
    conv_weight,
    conv_bias,
    proj_weight,
    dt_weight,
    dt_bias,
    a_log,
    skip_gain,
    leave_slot,
    dest_table,
    land_slot,
):
    slots, states, channels = ssm_state.shape
    mig = leave_slot.shape[1]
    taps = conv_state.shape[1]
    rank = dt_weight.shape[0]
    peers = n - 1
    cap = max(2, (mig + n - 2) // (n - 1))
    movers = peers * cap
    stays = slots - mig
    chunks = 16 // math.gcd(16, taps * cap)
    rows = chunks * taps * cap
    width = channels // chunks
    smem = pl.BlockSpec(memory_space=pltpu.SMEM)
    vmem = pl.BlockSpec(memory_space=pltpu.VMEM)
    anywhere = pl.BlockSpec(memory_space=pl.ANY)
    hbm = pl.BlockSpec(memory_space=pltpu.HBM)
    shape = jax.ShapeDtypeStruct
    def far(value):
        return pltpu.with_memory_space_constraint(value, pltpu.HBM)

    own = lax.axis_index("inst").astype(jnp.int32).reshape(1)
    conv_t = jnp.transpose(conv_state, (1, 0, 2))
    proj_t = proj_weight.T
    cols = proj_t.shape[0]
    padded = rank + LANES
    bias_row = conv_bias.reshape(1, channels)
    dt_bias_row = dt_bias.reshape(1, channels)
    skip_row = skip_gain.reshape(1, channels)

    with jax.named_scope("gather_conv"):
        *conv_sent, near, leave_tab = pl.pallas_call(
            functools.partial(gather_conv_kernel, n, cap, chunks),
            out_shape=[shape((rows, width), BF16)] * peers
            + [shape((cap, states, channels), BF16), shape((n * cap,), jnp.int32)],
            in_specs=[smem] + [hbm] * 4,
            out_specs=[vmem] * (peers + 1) + [smem],
            scratch_shapes=[
                pltpu.SMEM(leave_slot.shape, jnp.int32),
                pltpu.SMEM(dest_table.shape, jnp.int32),
                pltpu.VMEM((taps, slots, channels), BF16),
                pltpu.SemaphoreType.DMA((chunks + 2,)),
                pltpu.SemaphoreType.DMA((1, cap)),
            ],
            compiler_params=params(16),
        )(own, far(leave_slot), far(dest_table), far(conv_t), far(ssm_state))

    order = sorted(range(1, n), key=lambda k: -k)
    conv_got, ssm_got = {}, {}
    for k in order:
        conv_got[k] = exchange(conv_sent[k - 1], "inst", k, n)
    ssm_got[1] = exchange(near, "inst", 1, n)

    far_peers = list(range(2, n))
    with jax.named_scope("gather_ssm"):
        *ssm_sent, land_tab, stay_tab = pl.pallas_call(
            functools.partial(gather_ssm_kernel, n, cap, far_peers),
            out_shape=[shape((cap, states, channels), BF16)] * len(far_peers)
            + [shape((n * cap + 1,), jnp.int32), shape((slots,), jnp.int32)],
            in_specs=[smem] * 2 + [hbm] * 4 + [anywhere],
            out_specs=[vmem] * len(far_peers) + [smem, smem],
            scratch_shapes=[
                pltpu.SMEM(leave_slot.shape, jnp.int32),
                pltpu.SMEM(dest_table.shape, jnp.int32),
                pltpu.SMEM(land_slot.shape, jnp.int32),
                pltpu.SMEM((slots,), jnp.int32),
                pltpu.SemaphoreType.DMA((len(far_peers), cap)),
                pltpu.SemaphoreType.DMA((3,)),
            ],
            compiler_params=params(16),
        )(own, leave_tab, far(leave_slot), far(dest_table), far(land_slot), far(ssm_state), conv_got[1])
    for k in reversed(far_peers):
        ssm_got[k] = exchange(ssm_sent[k - 2], "inst", k, n)

    both = 2 * slots
    with jax.named_scope("project"):
        conv_out, new_conv, own_sum, send_sum = pl.pallas_call(
            functools.partial(project_kernel, n, cap, chunks),
            out_shape=[
                shape((both, channels), F32),
                shape((taps, slots, channels), BF16),
                shape((both, padded), F32),
                shape((both, padded), BF16),
            ],
            in_specs=[smem, anywhere] + [vmem] * (peers + 5),
            out_specs=[vmem, hbm, vmem, vmem],
            scratch_shapes=[pltpu.VMEM((slots, channels), BF16), pltpu.SemaphoreType.DMA((3,))],
            compiler_params=params(20),
            cost_estimate=cost(10**12),
        )(
            land_tab,
            ssm_got[1],
            *[conv_got[k] for k in range(1, n)],
            conv_t,
            x_new,
            conv_weight,
            bias_row,
            proj_t,
        )

    sums_got = [exchange(send_sum, "tp", k, tps) for k in range(tps - 1, 0, -1)]

    with jax.named_scope("gate"):
        ssm_held, weight_held, gate, skipped, rate, conv_m, skip_m, gate_m = pl.pallas_call(
            functools.partial(gate_kernel, n, cap),
            out_shape=[
                shape((slots, states, channels), BF16),
                shape((rank, channels), BF16),
            ]
            + [shape((both, channels), F32)] * 2
            + [shape((states, channels), F32)]
            + [shape((2 * movers, channels), F32)] * 3,
            in_specs=[smem] + [vmem] * 4 + [hbm] * 2,
            out_specs=[vmem] * 8,
            scratch_shapes=[pltpu.SemaphoreType.DMA((2,))],
            compiler_params=params(20),
        )(
            land_tab,
            conv_out,
            z_new.reshape(both, channels),
            skip_row,
            a_log,
            far(ssm_state),
            far(dt_weight),
        )

    step = min(512, channels)
    pad = -(-movers // 16) * 16
    with jax.named_scope("update_staying"):
        new_ssm, out_stay, size_m, drive_m, b_m, c_m = pl.pallas_call(
            functools.partial(stay_kernel, n, tps, cap, stays, step),
            out_shape=[
                shape((slots, states, channels), BF16),
                shape((both, channels), BF16),
                shape((2 * movers, channels), F32),
                shape((2 * movers, channels), F32),
                shape((2 * movers, states, LANES), F32),
                shape((2, 2 * pad, movers * states), BF16),
            ],
            in_specs=[smem, smem] + [vmem] * (tps + 8),
            out_specs=[hbm] + [vmem] * 5,
            scratch_shapes=[
                pltpu.VMEM((both, states, LANES), F32),
                pltpu.VMEM((2, both, slots * states), BF16),
                pltpu.VMEM((both, step), F32),
                pltpu.VMEM((both, step), F32),
                pltpu.VMEM((slots, states, step), BF16),
                pltpu.VMEM((channels // step, slots, states, step), BF16),
                pltpu.SemaphoreType.DMA((channels // step,)),
            ],
            compiler_params=params(24),
        )(
            land_tab,
            stay_tab,
            own_sum,
            *sums_got,
            weight_held,
            dt_bias_row,
            rate,
            conv_out,
            skipped,
            gate,
            conv_m,
            ssm_held,
        )

    parts = channels // step
    with jax.named_scope("update_arrived"):
        outputs, new_ssm = pl.pallas_call(
            functools.partial(arrive_kernel, n, cap, mig, step),
            out_shape=[shape((2, slots, channels), BF16), shape((slots, states, channels), BF16)],
            in_specs=[smem] + [vmem] * (peers + 8) + [hbm],
            out_specs=[hbm, hbm],
            scratch_shapes=[
                pltpu.VMEM((movers, states, step), BF16),
                pltpu.VMEM((parts, movers, states, step), BF16),
                pltpu.VMEM((2, pad, step), F32),
                pltpu.VMEM((parts, 2, slots, step), BF16),
                pltpu.SemaphoreType.DMA((parts, movers)),
                pltpu.SemaphoreType.DMA((parts,)),
            ],
            input_output_aliases={1 + peers + 8: 1},
            compiler_params=params(20),
        )(
            land_tab,
            *[ssm_got[k] for k in range(1, n)],
            rate,
            size_m,
            drive_m,
            skip_m,
            gate_m,
            b_m,
            c_m,
            out_stay,
            new_ssm,
        )
    return outputs, new_ssm, jnp.transpose(new_conv, (1, 0, 2))


def solution(mesh):
    return jax.shard_map(
        functools.partial(local, mesh.shape["inst"], mesh.shape["tp"]),
        mesh=mesh,
        in_specs=(
            P(None, ("groups", "inst"), "tp"),
            P(None, ("groups", "inst"), "tp"),
            P(("groups", "inst"), None, "tp"),
            P(("groups", "inst"), None, "tp"),
            P(None, "tp"),
            P("tp"),
            P("tp", None),
            P(None, "tp"),
            P("tp"),
            P(None, "tp"),
            P("tp"),
            P(("groups", "inst"), None),
            P("groups", None),
            P(("groups", "inst"), None),
        ),
        out_specs=(
            P(None, ("groups", "inst"), "tp"),
            P(("groups", "inst"), None, "tp"),
            P(("groups", "inst"), None, "tp"),
        ),
        check_vma=False,
    )
```

time: 145 us -> 50.7 us (0.35)
  local copies, waits for them, and re-layouts: 45.5 us -> 0.06 us
  Pallas kernels: 0 us -> 34.5 us
  waiting for transfers between devices: 37.3 us -> 5.25 us
  other arithmetic: 24.5 us -> 0.01 us
  between operations: 14.4 us -> 0.83 us
  matrix products: 13.5 us -> 0 us
    psum x1 -> x0, waiting for transfers between devices: 37.3 us -> none  [local(): summed = lax.psum(partial_sum, 'tp')]
    pallas_call x0 -> x6, Pallas kernels: none -> 34.5 us  [the longest x1 12.2 us: local(): pl.pallas_call(functools.partial(stay_kernel, n, tps, cap, stays, step),...]
    scatter x6 -> x0, local copies, waits for them, and re-layouts: 24.2 us -> none  [the longest x1 6.68 us: local(): conv_state.at[flat_target]]
    reduce_sum x3 -> x0, other arithmetic: 16.1 us -> none  [the longest x1 14.7 us: local(): jnp.sum(c_part[:, :, None] * hidden, axis=1) + skip_gain * conv_out]
    dot_general x4 -> x0, matrix products: 13.5 us -> none  [the longest x2 7.44 us: local(): jnp.dot(conv_out.astype(jnp.bfloat16), proj_weight, preferred_element_typ...]
    ppermute x0 -> x9, starting transfers between devices: none -> 9.88 us  [exchange(): return lax.ppermute(value, axis, [(i, i ^ k) for i in range(n)])]
    all_to_all x2 -> x0, starting transfers between devices: 8.69 us -> none  [the longest x1 4.45 us: local(): lax.all_to_all(buf_ssm, 'inst', split_axis=0, concat_axis=0, tiled=True)]
    unnamed x52 -> x20, local copies, waits for them, and re-layouts: 7.71 us -> 0.06 us
  transfers between devices with their start and end apart: 3 -> 9, of which waited for: 1 -> 2; matrix products, arithmetic and copies ran while one was open for 34% -> 0% of each run, Pallas kernels for 0% -> 48%
where the time goes in v2:
time: 50.7 us; the launch traced here: 50.5 us
  Pallas kernels  34.5 us (68%)
  starting transfers between devices  9.88 us (19%)
  waiting for transfers between devices  5.25 us (10%)
  between operations  0.83 us (2%)
    pallas_call x1, Pallas kernels, local(): pl.pallas_call(functools.partial(stay_kernel, n, tps, cap, stays, step),...  12.2 us
    ppermute x9, starting transfers between devices, exchange(): return lax.ppermute(value, axis, [(i, i ^ k) for i in range(n)])  9.88 us
    pallas_call x1, Pallas kernels, local(): pl.pallas_call(functools.partial(arrive_kernel, n, cap, mig, step), out_s...  7.24 us
    ppermute x9, waiting for transfers between devices, exchange(): return lax.ppermute(value, axis, [(i, i ^ k) for i in range(n)])  5.25 us
    pallas_call x1, Pallas kernels, local(): pl.pallas_call(functools.partial(gate_kernel, n, cap), out_shape=[shape((...  4.57 us
    pallas_call x1, Pallas kernels, local(): pl.pallas_call(functools.partial(project_kernel, n, cap, chunks), out_sha...  4.34 us
    pallas_call x1, Pallas kernels, local(): pl.pallas_call(functools.partial(gather_conv_kernel, n, cap, chunks), out...  3.22 us
    pallas_call x1, Pallas kernels, local(): pl.pallas_call(functools.partial(gather_ssm_kernel, n, cap, far_peers), o...  2.91 us
  transfers between devices with their start and end apart: 9, of which 2 were waited for; matrix products, arithmetic and copies ran while one was open for 0% of the time, Pallas kernels for 48%

profile of v2, /device:TPU:0, one launch (start us, length us, event | category | flops | bytes accessed | tf_op | source)
XLA Modules:
  0.0 50.5 jit_solution(12672681405440315146)
XLA Ops:
  0.6 0.0 slice-start.1
  0.7 3.2 %gather_conv.1 = (bf16[48,1024]{1,0:T(8,128)(2,1)S(1)}, bf16[48,1024]{1,0:T(8,128)(2,1)S(1)}, bf16[48,1024]{1,0:T(8,128)(2,1)S(1)}, bf16[4,16,4096]{2,1,0:T(8,128)(2,1)S(1)}, s32[16]{0:T(128)S(1)}) custom-call(s32[1]{0:T(128)} %bitcast.own_ref, s32[1,12]{1,0:T(1,128)} %leave_hbm.3, s32[4,12]{1,0:T(4,128)} %dest_hbm.3, bf16[3,48,4096]{2,1,0:T(8,128)(2,1)} %bitcast.8, ...), custom_call_target="tpu_custom_call" | custom-call | tf_op jit(solution)/shard_map/gather_conv/pallas_call | solution.py:467
  3.9 0.0 copy-start
  3.9 0.0 copy-start.5
  3.9 0.0 copy-start.6
  3.9 0.0 copy-start.7
  3.9 0.5 %collective-permute-start.1 = (bf16[4,16,4096]{2,1,0:T(8,128)(2,1)S(1)}, bf16[4,16,4096]{2,1,0:T(8,128)(2,1)S(1)}, u32[]{:S(2)}, u32[]{:S(2)}) collective-permute-start(bf16[4,16,4096]{2,1,0:T(8,128)(2,1)S(1)} %get-tuple-element.35), channel_id=1, source_target_pairs={{0,4},{4,0},{8,12},{12,8},{1,5},{5,1},{9,13},{13,9},{2,6},{6,2},{1... | collective-permute-start | bytes 1572872 | tf_op jit(solution)/shard_map/ppermute | solution.py:409
  4.4 0.1 collective-permute-start
  4.5 2.9 %collective-permute-start.4 = (bf16[48,1024]{1,0:T(8,128)(2,1)S(1)}, bf16[48,1024]{1,0:T(8,128)(2,1)S(1)}, u32[]{:S(2)}, u32[]{:S(2)}) collective-permute-start(bf16[48,1024]{1,0:T(8,128)(2,1)S(1)} %get-tuple-element.38), channel_id=1, source_target_pairs={{0,8},{4,12},{8,0},{12,4},{1,9},{5,13},{9,1},{13,5},{2,10},{6,14},... | collective-permute-start | bytes 294920 | tf_op jit(solution)/shard_map/ppermute | solution.py:409
  7.5 2.9 %gather_ssm.1 = (bf16[4,16,4096]{2,1,0:T(8,128)(2,1)}, bf16[4,16,4096]{2,1,0:T(8,128)(2,1)}, s32[17]{0:T(128)S(1)}, s32[48]{0:T(128)S(1)}) custom-call(s32[1]{0:T(128)} %bitcast.own_ref, s32[16]{0:T(128)S(1)} %get-tuple-element.32.leave_tab, s32[1,12]{1,0:T(1,128)} %leave_hbm.3, s32[4,12]{1,0:T(4,128)} %dest_hbm.3, s32[1,12]{1,0:T(1,128)} %land_hbm.1, ...), custom_call_target="tpu_custom_call" | custom-call | tf_op jit(solution)/shard_map/gather_ssm/pallas_call | solution.py:491
  10.4 1.6 %collective-permute-start.2 = (bf16[4,16,4096]{2,1,0:T(8,128)(2,1)}, bf16[4,16,4096]{2,1,0:T(8,128)(2,1)}, u32[]{:S(2)}, u32[]{:S(2)}) collective-permute-start(bf16[4,16,4096]{2,1,0:T(8,128)(2,1)} %get-tuple-element.36), channel_id=1, source_target_pairs={{0,8},{4,12},{8,0},{12,4},{1,9},{5,13},{9,1},{13,5},{2,10},{6,14},... | collective-permute-start | bytes 1572872 | tf_op jit(solution)/shard_map/ppermute | solution.py:409
  12.0 0.3 collective-permute-start.3
  12.3 0.3 collective-permute-done.5.rest_2_
  12.7 0.0 copy-start.1
  12.7 0.0 copy-start.2
  12.7 0.0 copy-start.3
  12.7 4.3 %project.1 = (f32[96,4096]{1,0:T(8,128)S(1)}, bf16[3,48,4096]{2,1,0:T(8,128)(2,1)}, f32[96,640]{1,0:T(8,128)S(1)}, bf16[96,640]{1,0:T(8,128)(2,1)S(1)}) custom-call(s32[17]{0:T(128)S(1)} %get-tuple-element.34.land_tab, bf16[4,16,4096]{2,1,0:T(8,128)(2,1)S(1)} %collective-permute-done.1._.rest_0_, bf16[48,1024]{1,0:T(8,128)(2,1)S(1)} %collective-permute-done._.rest_0_, ...), custom_call_target="tpu_custom_call" | custom-call | flops 999999995904 | tf_op jit(solution)/shard_map/project/pallas_call | solution.py:512
  17.1 1.6 %collective-permute-start.8 = (bf16[96,640]{1,0:T(8,128)(2,1)S(1)}, bf16[96,640]{1,0:T(8,128)(2,1)S(1)}, u32[]{:S(2)}, u32[]{:S(2)}) collective-permute-start(bf16[96,640]{1,0:T(8,128)(2,1)S(1)} %get-tuple-element.44), channel_id=1, source_target_pairs={{0,1},{1,0},{2,3},{3,2},{4,5},{5,4},{6,7},{7,6},{8,9},{9,8},{10,11... | collective-permute-start | bytes 368648 | tf_op jit(solution)/shard_map/ppermute | solution.py:409
  18.6 2.6 %collective-permute-start.7 = (bf16[96,640]{1,0:T(8,128)(2,1)S(1)}, bf16[96,640]{1,0:T(8,128)(2,1)S(1)}, u32[]{:S(2)}, u32[]{:S(2)}) collective-permute-start(bf16[96,640]{1,0:T(8,128)(2,1)S(1)} %get-tuple-element.44), channel_id=1, source_target_pairs={{0,2},{1,3},{2,0},{3,1},{4,6},{5,7},{6,4},{7,5},{8,10},{9,11},{10,... | collective-permute-start | bytes 368648 | tf_op jit(solution)/shard_map/ppermute | solution.py:409
  21.2 0.3 collective-permute-start.6
  21.5 4.6 %gate.1 = (bf16[48,16,4096]{2,1,0:T(8,128)(2,1)S(1)}, bf16[512,4096]{1,0:T(8,128)(2,1)S(1)}, f32[96,4096]{1,0:T(8,128)S(1)}, f32[96,4096]{1,0:T(8,128)S(1)}, f32...) custom-call(s32[17]{0:T(128)S(1)} %get-tuple-element.34.land_tab, ...), custom_call_target="tpu_custom_call" | custom-call | tf_op jit(solution)/shard_map/gate/pallas_call | solution.py:539
  26.1 4.9 %collective-permute-done.7.rest_1_ = bf16[96,640]{1,0:T(8,128)(2,1)S(1)} collective-permute-done((bf16[96,640]{1,0:T(8,128)(2,1)S(1)}, bf16[96,640]{1,0:T(8,128)(2,1)S(1)}, u32[]{:S(2)}, u32[]{:S(2)}) %collective-permute-start.7) | collective-permute-done | bytes 122912 | tf_op jit(solution)/shard_map/ppermute | solution.py:409
  31.0 12.2 %update_staying.1 = (bf16[48,16,4096]{2,1,0:T(8,128)(2,1)}, bf16[96,4096]{1,0:T(8,128)(2,1)S(1)}, f32[24,4096]{1,0:T(8,128)S(1)}, f32[24,4096]{1,0:T(8,128)S(1)}...) custom-call(s32[17]{0:T(128)S(1)} %get-tuple-element.34.land_tab, s32[48]{0:T(128)S(1)} %get-tuple-element.42.stay_tab, ...), custom_call_target="tpu_custom_call" | custom-call | tf_op jit(solution)/shard_map/update_staying/pallas_call | solution.py:565
  43.3 7.2 %update_arrived.1 = (bf16[2,48,4096]{2,1,0:T(8,128)(2,1)}, bf16[48,16,4096]{2,1,0:T(8,128)(2,1)}) custom-call(s32[17]{0:T(128)S(1)} %get-tuple-element.34.land_tab, bf16[4,16,4096]{2,1,0:T(8,128)(2,1)S(1)} %collective-permute-done.1._.rest_0_, bf16[4,16,4096]{2,1,0:T(8,128)(2,1)} %collective-permute-done.2.rest_1_, ...), custom_call_target="tpu_custom_call", output_to_operand_aliasing={{1}: (12, {})} | custom-call | tf_op jit(solution)/shard_map/update_arrived/pallas_call | solution.py:604
  (21 shorter events, 0.0 us)
Async XLA Ops:
  0.6 12.0 %slice-start = ((s8[4456448]{0:T(1024)(128)(4,1)}), s8[4194304]{0:T(1024)(128)(4,1)S(1)}, s32[]{:S(2)}) async-start(s8[4456448]{0:T(1024)(128)(4,1)} %bitcast.13), calls=%async_computation | async-start | bytes 8388608
  0.6 12.0 %slice-start.1 = ((s8[4456448]{0:T(1024)(128)(4,1)}), s8[262144]{0:T(1024)(128)(4,1)S(1)}, s32[]{:S(2)}) async-start(s8[4456448]{0:T(1024)(128)(4,1)} %bitcast.13), calls=%async_computation.1 | async-start | bytes 524288
  3.9 8.7 %copy-start = (bf16[48,3,4096]{2,0,1:T(8,128)(2,1)S(1)}, bf16[48,3,4096]{2,0,1:T(8,128)(2,1)}, u32[]{:S(2)}) copy-start(bf16[48,3,4096]{2,0,1:T(8,128)(2,1)} %param.17) | copy-start | bytes 3538948
  3.9 8.7 %copy-start.5 = (bf16[2,48,4096]{2,1,0:T(8,128)(2,1)S(1)}, bf16[2,48,4096]{2,1,0:T(8,128)(2,1)}, u32[]{:S(2)}) copy-start(bf16[2,48,4096]{2,1,0:T(8,128)(2,1)} %rest_4_.1) | copy-start | bytes 2359300
  3.9 8.7 %copy-start.6 = (f32[4,4096]{1,0:T(4,128)S(1)}, f32[4,4096]{1,0:T(4,128)}, u32[]{:S(2)}) copy-start(f32[4,4096]{1,0:T(4,128)} %rest_5_.1) | copy-start | bytes 196612
  3.9 8.7 %copy-start.7 = (f32[4096]{0:T(1024)S(1)}, f32[4096]{0:T(1024)}, u32[]{:S(2)}) copy-start(f32[4096]{0:T(1024)} %param.19) | copy-start | bytes 49156
  3.9 8.7 %collective-permute-start.1 = (bf16[4,16,4096]{2,1,0:T(8,128)(2,1)S(1)}, bf16[4,16,4096]{2,1,0:T(8,128)(2,1)S(1)}, u32[]{:S(2)}, u32[]{:S(2)}) collective-permute-start(bf16[4,16,4096]{2,1,0:T(8,128)(2,1)S(1)} %get-tuple-element.35), channel_id=1, source_target_pairs={{0,4},{4,0},{8,12},{12,8},{1,5},{5,1},{9,13},{13,9},{2,6},{6,2},{1... | collective-permute-start | bytes 1572872 | tf_op jit(solution)/shard_map/ppermute | solution.py:409
  4.4 3.0 %collective-permute-start = (bf16[48,1024]{1,0:T(8,128)(2,1)S(1)}, bf16[48,1024]{1,0:T(8,128)(2,1)S(1)}, u32[]{:S(2)}, u32[]{:S(2)}) collective-permute-start(bf16[48,1024]{1,0:T(8,128)(2,1)S(1)} %get-tuple-element.33), channel_id=1, source_target_pairs={{0,4},{4,0},{8,12},{12,8},{1,5},{5,1},{9,13},{13,9},{2,6},{6,2},{1... | collective-permute-start | bytes 294920 | tf_op jit(solution)/shard_map/ppermute | solution.py:409
  4.5 7.8 %collective-permute-start.4 = (bf16[48,1024]{1,0:T(8,128)(2,1)S(1)}, bf16[48,1024]{1,0:T(8,128)(2,1)S(1)}, u32[]{:S(2)}, u32[]{:S(2)}) collective-permute-start(bf16[48,1024]{1,0:T(8,128)(2,1)S(1)} %get-tuple-element.38), channel_id=1, source_target_pairs={{0,8},{4,12},{8,0},{12,4},{1,9},{5,13},{9,1},{13,5},{2,10},{6,14},... | collective-permute-start | bytes 294920 | tf_op jit(solution)/shard_map/ppermute | solution.py:409
  7.5 5.1 %collective-permute-start.5 = (bf16[48,1024]{1,0:T(8,128)(2,1)S(1)}, bf16[48,1024]{1,0:T(8,128)(2,1)S(1)}, u32[]{:S(2)}, u32[]{:S(2)}) collective-permute-start(bf16[48,1024]{1,0:T(8,128)(2,1)S(1)} %get-tuple-element.39), channel_id=1, source_target_pairs={{0,12},{4,8},{8,4},{12,0},{1,13},{5,9},{9,5},{13,1},{2,14},{6,10},... | collective-permute-start | bytes 294920 | tf_op jit(solution)/shard_map/ppermute | solution.py:409
  10.4 32.9 %collective-permute-start.2 = (bf16[4,16,4096]{2,1,0:T(8,128)(2,1)}, bf16[4,16,4096]{2,1,0:T(8,128)(2,1)}, u32[]{:S(2)}, u32[]{:S(2)}) collective-permute-start(bf16[4,16,4096]{2,1,0:T(8,128)(2,1)} %get-tuple-element.36), channel_id=1, source_target_pairs={{0,8},{4,12},{8,0},{12,4},{1,9},{5,13},{9,1},{13,5},{2,10},{6,14},... | collective-permute-start | bytes 1572872 | tf_op jit(solution)/shard_map/ppermute | solution.py:409
  12.0 31.3 %collective-permute-start.3 = (bf16[4,16,4096]{2,1,0:T(8,128)(2,1)}, bf16[4,16,4096]{2,1,0:T(8,128)(2,1)}, u32[]{:S(2)}, u32[]{:S(2)}) collective-permute-start(bf16[4,16,4096]{2,1,0:T(8,128)(2,1)} %get-tuple-element.37), channel_id=1, source_target_pairs={{0,12},{4,8},{8,4},{12,0},{1,13},{5,9},{9,5},{13,1},{2,14},{6,10},... | collective-permute-start | bytes 1572872 | tf_op jit(solution)/shard_map/ppermute | solution.py:409
  12.7 8.8 %copy-start.1 = (bf16[2,48,4096]{2,1,0:T(8,128)(2,1)S(1)}, bf16[2,48,4096]{2,1,0:T(8,128)(2,1)}, u32[]{:S(2)}) copy-start(bf16[2,48,4096]{2,1,0:T(8,128)(2,1)} %param.15) | copy-start | bytes 2359300
  12.7 8.8 %copy-start.2 = (f32[16,4096]{1,0:T(8,128)S(1)}, f32[16,4096]{1,0:T(8,128)}, u32[]{:S(2)}) copy-start(f32[16,4096]{1,0:T(8,128)} %a_log.1) | copy-start | bytes 786436
  12.7 8.8 %copy-start.3 = (f32[4096]{0:T(1024)S(1)}, f32[4096]{0:T(1024)}, u32[]{:S(2)}) copy-start(f32[4096]{0:T(1024)} %param.24) | copy-start | bytes 49156
  17.1 9.0 %collective-permute-start.8 = (bf16[96,640]{1,0:T(8,128)(2,1)S(1)}, bf16[96,640]{1,0:T(8,128)(2,1)S(1)}, u32[]{:S(2)}, u32[]{:S(2)}) collective-permute-start(bf16[96,640]{1,0:T(8,128)(2,1)S(1)} %get-tuple-element.44), channel_id=1, source_target_pairs={{0,1},{1,0},{2,3},{3,2},{4,5},{5,4},{6,7},{7,6},{8,9},{9,8},{10,11... | collective-permute-start | bytes 368648 | tf_op jit(solution)/shard_map/ppermute | solution.py:409
  18.6 12.4 %collective-permute-start.7 = (bf16[96,640]{1,0:T(8,128)(2,1)S(1)}, bf16[96,640]{1,0:T(8,128)(2,1)S(1)}, u32[]{:S(2)}, u32[]{:S(2)}) collective-permute-start(bf16[96,640]{1,0:T(8,128)(2,1)S(1)} %get-tuple-element.44), channel_id=1, source_target_pairs={{0,2},{1,3},{2,0},{3,1},{4,6},{5,7},{6,4},{7,5},{8,10},{9,11},{10,... | collective-permute-start | bytes 368648 | tf_op jit(solution)/shard_map/ppermute | solution.py:409
  21.2 9.8 %collective-permute-start.6 = (bf16[96,640]{1,0:T(8,128)(2,1)S(1)}, bf16[96,640]{1,0:T(8,128)(2,1)S(1)}, u32[]{:S(2)}, u32[]{:S(2)}) collective-permute-start(bf16[96,640]{1,0:T(8,128)(2,1)S(1)} %get-tuple-element.44), channel_id=1, source_target_pairs={{0,3},{1,2},{2,1},{3,0},{4,7},{5,6},{6,5},{7,4},{8,11},{9,10},{10,... | collective-permute-start | bytes 368648 | tf_op jit(solution)/shard_map/ppermute | solution.py:409
  21.5 9.5 %copy-start.4 = (f32[4096]{0:T(1024)S(1)}, f32[4096]{0:T(1024)}, u32[]{:S(2)}) copy-start(f32[4096]{0:T(1024)} %param.22) | copy-start | bytes 49156

commit v3 on v2

--- a/solution.py
+++ b/solution.py
@@ -13,6 +13,7 @@
 LANES = 128
 LOG2E = math.log2(math.e)
 MIB = 1 << 20
+PIECE = 512
 
 
 def iota(shape, dim):
@@ -223,11 +224,11 @@
     return both.reshape(rows, states, LANES)
 
 
-def spread_diagonal(values, lane, states, rows):
-    cols = rows * states
+def spread_diagonal(values, lane, states, owner):
+    cols = owner.shape[1]
     pick = iota((LANES, cols), 0) == lax.rem(iota((LANES, cols), 1), states) + lane
     pick = jnp.where(pick, 1.0, 0.0).astype(BF16)
-    keep = lax.div(iota((values.shape[0], cols), 1), states) == iota((values.shape[0], cols), 0)
+    keep = owner == iota((values.shape[0], cols), 0)
     high = values.astype(BF16)
     low = (values - high.astype(F32)).astype(BF16)
     parts = [jnp.where(keep, jnp.dot(v, pick, preferred_element_type=F32), 0.0) for v in (high, low)]
@@ -248,9 +249,7 @@
     return jnp.concatenate([tile] * (lanes // LANES), axis=1)
 
 
-def gate_kernel(n, cap, land_tab, conv_out, z_new, skip, a_log, ssm, dt_weight, *rest):
-    ssm_held, weight_held, gate, skipped, rate, conv_m, skip_m, gate_m, sems = rest
-    slots = conv_out.shape[0] // 2
+def gate_kernel(conv_out, z_new, skip, a_log, ssm, dt_weight, ssm_held, weight_held, gate, skipped, rate, sems):
     held = [
         pltpu.make_async_copy(ssm, ssm_held, sems.at[0]),
         pltpu.make_async_copy(dt_weight, weight_held, sems.at[1]),
@@ -260,26 +259,30 @@
     gate[...] = silu(z_new[...].astype(F32))
     skipped[...] = skip[...] * conv_out[...]
     rate[...] = -LOG2E * jnp.exp(a_log[...])
-    movers = (n - 1) * cap
-    for t in range(2):
-        for i in range(movers):
-            from_row = pl.ds(t * slots + jnp.maximum(land_tab[cap + i], 0), 1)
-            at = t * movers + i
-            for ref, source in ((conv_m, conv_out), (skip_m, skipped), (gate_m, gate)):
-                ref[at : at + 1, :] = source[from_row, :]
     for copy in held:
         copy.wait()
 
 
+def both_steps(slot, slots, before, place, rate_ref, size, drive, b_all, middle, fresh):
+    b_rows = [b_all[t * slots + slot] for t in range(2)]
+    for start in range(0, rate_ref.shape[1], PIECE):
+        lanes = slice(start, start + PIECE)
+        rate = rate_ref[:, lanes]
+        hidden = before(lanes).astype(F32)
+        for t, after in ((0, middle), (1, fresh)):
+            at = pl.ds(t * slots + slot, 1)
+            hidden = advance(hidden, rate, size[at, lanes], drive[at, lanes], wide(b_rows[t], PIECE))
+            after[place, :, lanes] = hidden.astype(BF16)
+
+
 def stay_kernel(n, tps, cap, stays, step, land_tab, stay_tab, own_sum, *rest):
     got = rest[: tps - 1]
-    dt_weight, dt_bias, rate_ref, conv_out, skipped, gate, conv_m, ssm = rest[tps - 1 : tps + 7]
-    new_ssm, out, size_m, drive_m, b_m, c_m = rest[tps + 7 : tps + 13]
-    b_all, c_all, size_s, drive_s, middle, fresh, sems = rest[tps + 13 :]
+    dt_weight, dt_bias, rate_ref, conv_out, near, ssm = rest[tps - 1 : tps + 5]
+    new_ssm, size_s, drive_s, b_all, c_all, c_far, middle, fresh, sems = rest[tps + 5 :]
     rank = dt_weight.shape[0]
     states, channels = rate_ref.shape
     slots = ssm.shape[0]
-    movers = (n - 1) * cap
+    far = (n - 2) * cap
 
     raw = own_sum[:, :rank]
     tail = own_sum[:, rank:]
@@ -289,120 +292,105 @@
         tail += piece + pltpu.roll(piece, LANES - 2 * states, 1)
     scale = lax.rsqrt(jnp.mean(raw * raw, axis=1, keepdims=True) + 1e-06)
     normed = (raw * scale).astype(BF16)
+    for start in range(0, channels, step):
+        lanes = slice(start, start + step)
+        pre = jnp.dot(normed, dt_weight[:, lanes], preferred_element_type=F32) + dt_bias[:, lanes]
+        size = jnp.maximum(pre, 0.0) + jnp.log1p(jnp.exp(-jnp.abs(pre)))
+        size_s[:, lanes] = size
+        drive_s[:, lanes] = size * conv_out[:, lanes]
     b_all[...] = spread(tail, 0, states)
-    middle[...] = jnp.zeros_like(middle)
-    pad = c_m.shape[1] // 2
-    row = iota((pad, slots), 0)
-    slot_of = jnp.full(row.shape, -1, jnp.int32)
-    for i in range(movers):
-        slot_of = jnp.where(row == i, land_tab[cap + i], slot_of)
-    pick = jnp.where(slot_of == iota((pad, slots), 1), 1.0, 0.0)
+    col = lax.div(iota((1, slots * states), 1), states)
+    far_col = lax.div(iota((1, far * states), 1), states)
+    far_slot = jnp.full(far_col.shape, -1, jnp.int32)
+    for i in range(far):
+        far_slot = jnp.where(far_col == i, land_tab[2 * cap + i], far_slot)
     for t in range(2):
         mine = tail[t * slots : (t + 1) * slots]
-        c_all[t] = spread_diagonal(mine, states, states, slots)
-        moved = jnp.dot(pick, mine, preferred_element_type=F32, precision=lax.Precision.HIGHEST)
-        c_m[t] = spread_diagonal(moved, states, states, movers)
-        for i in range(movers):
-            b_m[t * movers + i] = b_all[t * slots + jnp.maximum(land_tab[cap + i], 0)]
-
-    def store(place, lanes):
-        return pltpu.make_async_copy(fresh.at[place], new_ssm.at[:, :, lanes], sems.at[place])
-
-    def chunk(place, _):
-        lanes = pl.ds(pl.multiple_of(place * step, step), step)
-        pre = jnp.dot(normed, dt_weight[:, lanes], preferred_element_type=F32) + dt_bias[:, lanes]
-        size = jnp.maximum(pre, 0.0) + jnp.log1p(jnp.exp(-jnp.abs(pre)))
-        size_s[...] = size
-        drive_s[...] = size * conv_out[:, lanes]
-        rate = rate_ref[:, lanes]
-
-        for i in range(movers):
-            fresh[place, jnp.maximum(land_tab[cap + i], 0)] = jnp.zeros((states, step), BF16)
-
-        def one(i, _):
-            slot = stay_tab[i]
-            hidden = ssm[slot, :, lanes].astype(F32)
-            for t, after in ((0, middle.at[slot]), (1, fresh.at[place, slot])):
-                at = pl.ds(t * slots + slot, 1)
-                hidden = advance(hidden, rate, size_s[at, :], drive_s[at, :], wide(b_all[t * slots + slot], step))
-                after[...] = hidden.astype(BF16)
+        c_all[t] = spread_diagonal(mine, states, states, col)
+        c_far[t] = spread_diagonal(mine, states, states, far_slot)
+    for i in range(far):
+        slot = jnp.maximum(land_tab[2 * cap + i], 0)
+        middle[slot] = jnp.zeros((states, channels), BF16)
+        fresh[slot] = jnp.zeros((states, channels), BF16)
+
+    def store(slot, i):
+        return pltpu.make_async_copy(fresh.at[slot], new_ssm.at[slot], sems.at[i])
+
+    def update(slot, before, i):
+        both_steps(slot, slots, before, slot, rate_ref, size_s, drive_s, b_all, middle, fresh)
+        store(slot, i).start()
+
+    def stay(i, _):
+        slot = stay_tab[i]
+        update(slot, lambda lanes: ssm[slot, :, lanes], i)
+        return 0
+
+    def arrive(i, _):
+        slot = land_tab[cap + i]
+
+        @pl.when(slot >= 0)
+        def _():
+            update(slot, lambda lanes: near[i, :, lanes], stays + i)
+
+        return 0
+
+    lax.fori_loop(0, stays, stay, 0)
+    lax.fori_loop(0, cap, arrive, 0)
+    for i in range(stays):
+        store(stay_tab[i], i).wait()
+    for i in range(cap):
+        pl.when(land_tab[cap + i] >= 0)(store(land_tab[cap + i], stays + i).wait)
+
+
+def arrive_kernel(n, cap, full, step, land_tab, *rest):
+    far_peers = n - 2
+    got = rest[:far_peers]
+    rate_ref, size, drive, b_all, c_all, c_far, middle, fresh, skipped, gate, _ = rest[far_peers : far_peers + 11]
+    out, new_ssm, held, mid_far, new_far, total, done_s, got_sems, sems, out_sems = rest[far_peers + 11 :]
+    channels = rate_ref.shape[1]
+    far = far_peers * cap
+    slots = out.shape[1]
+    loads = [pltpu.make_async_copy(g, held.at[at], got_sems.at[at]) for at, g in enumerate(got)]
+    for load in loads:
+        load.start()
+
+    def copy(i):
+        return pltpu.make_async_copy(new_far.at[i], new_ssm.at[land_tab[2 * cap + i]], sems.at[i])
+
+    def copy_out(place):
+        lanes = pl.ds(place * step, step)
+        return pltpu.make_async_copy(done_s.at[:, :, lanes], out.at[:, :, lanes], out_sems.at[place])
+
+    parts = [slice(start, start + step) for start in range(0, channels, step)]
+    for lanes in parts:
+        for t, after in ((0, middle), (1, fresh)):
+            total[t * slots : (t + 1) * slots, lanes] = read(c_all[t], after[:, :, lanes])
+    for at, load in enumerate(loads):
+        load.wait()
+
+        def one(s, _, at=at):
+            i = at * cap + s
+            slot = land_tab[2 * cap + i]
+
+            def before(lanes):
+                state = held[at, s, :, lanes]
+                return state if far + cap == full else jnp.where(slot >= 0, state, jnp.zeros_like(state))
+
+            both_steps(jnp.maximum(slot, 0), slots, before, i, rate_ref, size, drive, b_all, mid_far, new_far)
+            pl.when(slot >= 0)(copy(i).start)
             return 0
 
-        lax.fori_loop(0, stays, one, 0, unroll=4)
-        store(place, lanes).start()
-        for t, after in ((0, middle[...]), (1, fresh[place])):
+        lax.fori_loop(0, cap, one, 0)
+    for place, lanes in enumerate(parts):
+        for t, after in ((0, mid_far), (1, new_far)):
             at = slice(t * slots, (t + 1) * slots)
-            out[at, lanes] = ((read(c_all[t], after) + skipped[at, lanes]) * gate[at, lanes]).astype(BF16)
-        for t in range(2):
-            for i in range(movers):
-                from_row = pl.ds(t * slots + jnp.maximum(land_tab[cap + i], 0), 1)
-                at = t * movers + i
-                here = size_s[from_row, :]
-                size_m[at : at + 1, lanes] = here
-                drive_m[at : at + 1, lanes] = here * conv_m[at : at + 1, lanes]
-        return 0
-
-    lax.fori_loop(0, channels // step, chunk, 0)
-    for place in range(channels // step):
-        store(place, pl.ds(place * step, step)).wait()
-
-
-def arrive_kernel(n, cap, full, step, land_tab, *rest):
-    peers = n - 1
-    got = rest[:peers]
-    rate_ref, size_m, drive_m, skip_m, gate_m, b_m, c_m, out_in, _ = rest[peers : peers + 9]
-    out, new_ssm, middle, fresh, rows_s, done_s, sems, out_sems = rest[peers + 9 :]
-    states, channels = rate_ref.shape
-    movers = peers * cap
-    slots = out.shape[1]
-    pad = rows_s.shape[1]
-    row = iota((slots, pad), 0)
-    col = iota((1, pad), 1)
-    target = jnp.full(col.shape, -1, jnp.int32)
-    arrived = jnp.zeros((slots, 1), jnp.bool_)
-    slot_row = iota((slots, 1), 0)
-    for i in range(movers):
-        slot = land_tab[cap + i]
-        target = jnp.where(col == i, slot, target)
-        arrived = arrived | (slot_row == slot)
-    pick = jnp.where(row == target, 1.0, 0.0).astype(BF16)
-    rows_s[...] = jnp.zeros_like(rows_s)
-
-    def copy(i, lanes, place):
-        return pltpu.make_async_copy(fresh.at[place, i], new_ssm.at[land_tab[cap + i], :, lanes], sems.at[place, i])
-
-    def copy_out(lanes, place):
-        return pltpu.make_async_copy(done_s.at[place], out.at[:, :, lanes], out_sems.at[place])
-
-    def chunk(place, _):
-        lanes = pl.ds(pl.multiple_of(place * step, step), step)
-        rate = rate_ref[:, lanes]
-        for i in range(movers):
-            hidden = got[i // cap][i % cap, :, lanes].astype(F32)
-            if movers != full:
-                hidden = jnp.where(land_tab[cap + i] >= 0, hidden, 0.0)
-            for t, after in ((0, middle.at[i]), (1, fresh.at[place, i])):
-                at = slice(t * movers + i, t * movers + i + 1)
-                hidden = advance(hidden, rate, size_m[at, lanes], drive_m[at, lanes], wide(b_m[t * movers + i], step))
-                after[...] = hidden.astype(BF16)
-        for i in range(movers):
-            pl.when(land_tab[cap + i] >= 0)(copy(i, lanes, place).start)
-        for t in range(2):
-            after = middle[...] if t == 0 else fresh[place]
-            at = slice(t * movers, (t + 1) * movers)
-            rows_s[t, :movers, :] = (read(c_m[t], after)[:movers] + skip_m[at, lanes]) * gate_m[at, lanes]
-            placed = jnp.dot(pick, rows_s[t].astype(BF16), preferred_element_type=F32)
-            kept = out_in[t * slots : (t + 1) * slots, lanes].astype(F32)
-            done_s[place, t] = jnp.where(arrived, placed, kept).astype(BF16)
-        copy_out(lanes, place).start()
-        return 0
-
-    lax.fori_loop(0, channels // step, chunk, 0)
-    for place in range(channels // step):
-        lanes = pl.ds(place * step, step)
-        copy_out(lanes, place).wait()
-        for i in range(movers):
-            pl.when(land_tab[cap + i] >= 0)(copy(i, lanes, place).wait)
+            sums = total[at, lanes] + read(c_far[t], after[:, :, lanes])
+            done_s[t, :, lanes] = ((sums + skipped[at, lanes]) * gate[at, lanes]).astype(BF16)
+        copy_out(place).start()
+    for place in range(len(parts)):
+        copy_out(place).wait()
+    for i in range(far):
+        pl.when(land_tab[2 * cap + i] >= 0)(copy(i).wait)
 
 
 def exchange(value, axis, k, n):
@@ -536,54 +524,40 @@
     sums_got = [exchange(send_sum, "tp", k, tps) for k in range(tps - 1, 0, -1)]
 
     with jax.named_scope("gate"):
-        ssm_held, weight_held, gate, skipped, rate, conv_m, skip_m, gate_m = pl.pallas_call(
-            functools.partial(gate_kernel, n, cap),
+        ssm_held, weight_held, gate, skipped, rate = pl.pallas_call(
+            gate_kernel,
             out_shape=[
                 shape((slots, states, channels), BF16),
                 shape((rank, channels), BF16),
-            ]
-            + [shape((both, channels), F32)] * 2
-            + [shape((states, channels), F32)]
-            + [shape((2 * movers, channels), F32)] * 3,
-            in_specs=[smem] + [vmem] * 4 + [hbm] * 2,
-            out_specs=[vmem] * 8,
+                shape((both, channels), F32),
+                shape((both, channels), F32),
+                shape((states, channels), F32),
+            ],
+            in_specs=[vmem] * 4 + [hbm] * 2,
+            out_specs=[vmem] * 5,
             scratch_shapes=[pltpu.SemaphoreType.DMA((2,))],
             compiler_params=params(20),
-        )(
-            land_tab,
-            conv_out,
-            z_new.reshape(both, channels),
-            skip_row,
-            a_log,
-            far(ssm_state),
-            far(dt_weight),
-        )
-
-    step = min(512, channels)
-    pad = -(-movers // 16) * 16
+        )(conv_out, z_new.reshape(both, channels), skip_row, a_log, far(ssm_state), far(dt_weight))
+
+    step = min(1024, channels)
+    far_rows = (n - 2) * cap
     with jax.named_scope("update_staying"):
-        new_ssm, out_stay, size_m, drive_m, b_m, c_m = pl.pallas_call(
+        new_ssm, *state = pl.pallas_call(
             functools.partial(stay_kernel, n, tps, cap, stays, step),
             out_shape=[
                 shape((slots, states, channels), BF16),
-                shape((both, channels), BF16),
-                shape((2 * movers, channels), F32),
-                shape((2 * movers, channels), F32),
-                shape((2 * movers, states, LANES), F32),
-                shape((2, 2 * pad, movers * states), BF16),
+                shape((both, channels), F32),
+                shape((both, channels), F32),
+                shape((both, states, LANES), F32),
+                shape((2, both, slots * states), BF16),
+                shape((2, both, far_rows * states), BF16),
+                shape((slots, states, channels), BF16),
+                shape((slots, states, channels), BF16),
             ],
-            in_specs=[smem, smem] + [vmem] * (tps + 8),
-            out_specs=[hbm] + [vmem] * 5,
-            scratch_shapes=[
-                pltpu.VMEM((both, states, LANES), F32),
-                pltpu.VMEM((2, both, slots * states), BF16),
-                pltpu.VMEM((both, step), F32),
-                pltpu.VMEM((both, step), F32),
-                pltpu.VMEM((slots, states, step), BF16),
-                pltpu.VMEM((channels // step, slots, states, step), BF16),
-                pltpu.SemaphoreType.DMA((channels // step,)),
-            ],
-            compiler_params=params(24),
+            in_specs=[smem, smem] + [vmem] * (tps + 6),
+            out_specs=[hbm] + [vmem] * 7,
+            scratch_shapes=[pltpu.SemaphoreType.DMA((stays + cap,))],
+            compiler_params=params(20),
         )(
             land_tab,
             stay_tab,
@@ -593,9 +567,7 @@
             dt_bias_row,
             rate,
             conv_out,
-            skipped,
-            gate,
-            conv_m,
+            ssm_got[1],
             ssm_held,
         )
 
@@ -604,31 +576,21 @@
         outputs, new_ssm = pl.pallas_call(
             functools.partial(arrive_kernel, n, cap, mig, step),
             out_shape=[shape((2, slots, channels), BF16), shape((slots, states, channels), BF16)],
-            in_specs=[smem] + [vmem] * (peers + 8) + [hbm],
+            in_specs=[smem] + [anywhere] * (n - 2) + [vmem] * 10 + [hbm],
             out_specs=[hbm, hbm],
             scratch_shapes=[
-                pltpu.VMEM((movers, states, step), BF16),
-                pltpu.VMEM((parts, movers, states, step), BF16),
-                pltpu.VMEM((2, pad, step), F32),
-                pltpu.VMEM((parts, 2, slots, step), BF16),
-                pltpu.SemaphoreType.DMA((parts, movers)),
+                pltpu.VMEM((n - 2, cap, states, channels), BF16),
+                pltpu.VMEM((far_rows, states, channels), BF16),
+                pltpu.VMEM((far_rows, states, channels), BF16),
+                pltpu.VMEM((both, channels), F32),
+                pltpu.VMEM((2, slots, channels), BF16),
+                pltpu.SemaphoreType.DMA((n - 2,)),
+                pltpu.SemaphoreType.DMA((far_rows,)),
                 pltpu.SemaphoreType.DMA((parts,)),
             ],
-            input_output_aliases={1 + peers + 8: 1},
-            compiler_params=params(20),
-        )(
-            land_tab,
-            *[ssm_got[k] for k in range(1, n)],
-            rate,
-            size_m,
-            drive_m,
-            skip_m,
-            gate_m,
-            b_m,
-            c_m,
-            out_stay,
-            new_ssm,
-        )
+            input_output_aliases={1 + (n - 2) + 10: 1},
+            compiler_params=params(16),
+        )(land_tab, *[ssm_got[k] for k in range(2, n)], rate, *state, skipped, gate, new_ssm)
     return outputs, new_ssm, jnp.transpose(new_conv, (1, 0, 2))
 
 

time: 50.7 us -> 44.5 us (0.88)
  Pallas kernels: 34.5 us -> 27.8 us
  waiting for transfers between devices: 5.25 us -> 5.79 us
    pallas_call x1, Pallas kernels: 12.2 us -> 8.29 us  [local(): pl.pallas_call(functools.partial(stay_kernel, n, tps, cap, stays, step),...]
    pallas_call x1, Pallas kernels: 7.24 us -> 5.04 us  [local(): pl.pallas_call(functools.partial(arrive_kernel, n, cap, mig, step), out_s...]
    ppermute x9, waiting for transfers between devices: 5.25 us -> 5.79 us  [exchange(): return lax.ppermute(value, axis, [(i, i ^ k) for i in range(n)])]
    pallas_call x1, Pallas kernels: 4.57 us -> 4.03 us  [local(): pl.pallas_call(gate_kernel, out_shape=[shape((slots, states, channels), B...]
  transfers between devices with their start and end apart: 9 -> 9, of which waited for: 2 -> 2; matrix products, arithmetic and copies ran while one was open for 0% -> 0% of each run, Pallas kernels for 48% -> 44%
where the time goes in v3:
time: 44.5 us; the launch traced here: 44.4 us
  Pallas kernels  27.8 us (62%)
  starting transfers between devices  9.88 us (22%)
  waiting for transfers between devices  5.79 us (13%)
  between operations  0.83 us (2%)
    ppermute x9, starting transfers between devices, exchange(): return lax.ppermute(value, axis, [(i, i ^ k) for i in range(n)])  9.88 us
    pallas_call x1, Pallas kernels, local(): pl.pallas_call(functools.partial(stay_kernel, n, tps, cap, stays, step),...  8.29 us
    ppermute x9, waiting for transfers between devices, exchange(): return lax.ppermute(value, axis, [(i, i ^ k) for i in range(n)])  5.79 us
    pallas_call x1, Pallas kernels, local(): pl.pallas_call(functools.partial(arrive_kernel, n, cap, mig, step), out_s...  5.04 us
    pallas_call x1, Pallas kernels, local(): pl.pallas_call(functools.partial(project_kernel, n, cap, chunks), out_sha...  4.31 us
    pallas_call x1, Pallas kernels, local(): pl.pallas_call(gate_kernel, out_shape=[shape((slots, states, channels), B...  4.03 us
    pallas_call x1, Pallas kernels, local(): pl.pallas_call(functools.partial(gather_conv_kernel, n, cap, chunks), out...  3.22 us
    pallas_call x1, Pallas kernels, local(): pl.pallas_call(functools.partial(gather_ssm_kernel, n, cap, far_peers), o...  2.91 us
  transfers between devices with their start and end apart: 9, of which 2 were waited for; matrix products, arithmetic and copies ran while one was open for 0% of the time, Pallas kernels for 44%

profile of v3, /device:TPU:0, one launch (start us, length us, event | category | flops | bytes accessed | tf_op | source)
XLA Modules:
  0.0 44.4 jit_solution(4421351050049597217)
XLA Ops:
  0.6 0.0 slice-start.1
  0.7 3.2 %gather_conv.1 = (bf16[48,1024]{1,0:T(8,128)(2,1)S(1)}, bf16[48,1024]{1,0:T(8,128)(2,1)S(1)}, bf16[48,1024]{1,0:T(8,128)(2,1)S(1)}, bf16[4,16,4096]{2,1,0:T(8,128)(2,1)S(1)}, s32[16]{0:T(128)S(1)}) custom-call(s32[1]{0:T(128)} %bitcast.own_ref, s32[1,12]{1,0:T(1,128)} %leave_hbm.3, s32[4,12]{1,0:T(4,128)} %dest_hbm.3, bf16[3,48,4096]{2,1,0:T(8,128)(2,1)} %bitcast.8, ...), custom_call_target="tpu_custom_call" | custom-call | tf_op jit(solution)/shard_map/gather_conv/pallas_call | solution.py:455
  3.9 0.0 copy-start
  3.9 0.0 copy-start.5
  3.9 0.0 copy-start.6
  3.9 0.0 copy-start.7
  3.9 0.5 %collective-permute-start.3 = (bf16[4,16,4096]{2,1,0:T(8,128)(2,1)S(1)}, bf16[4,16,4096]{2,1,0:T(8,128)(2,1)S(1)}, u32[]{:S(2)}, u32[]{:S(2)}) collective-permute-start(bf16[4,16,4096]{2,1,0:T(8,128)(2,1)S(1)} %get-tuple-element.36), channel_id=1, source_target_pairs={{0,4},{4,0},{8,12},{12,8},{1,5},{5,1},{9,13},{13,9},{2,6},{6,2},{1... | collective-permute-start | bytes 1572872 | tf_op jit(solution)/shard_map/ppermute | solution.py:397
  4.4 0.1 collective-permute-start
  4.5 2.9 %collective-permute-start.4 = (bf16[48,1024]{1,0:T(8,128)(2,1)S(1)}, bf16[48,1024]{1,0:T(8,128)(2,1)S(1)}, u32[]{:S(2)}, u32[]{:S(2)}) collective-permute-start(bf16[48,1024]{1,0:T(8,128)(2,1)S(1)} %get-tuple-element.37), channel_id=1, source_target_pairs={{0,8},{4,12},{8,0},{12,4},{1,9},{5,13},{9,1},{13,5},{2,10},{6,14},... | collective-permute-start | bytes 294920 | tf_op jit(solution)/shard_map/ppermute | solution.py:397
  7.5 2.9 %gather_ssm.1 = (bf16[4,16,4096]{2,1,0:T(8,128)(2,1)}, bf16[4,16,4096]{2,1,0:T(8,128)(2,1)}, s32[17]{0:T(128)S(1)}, s32[48]{0:T(128)S(1)}) custom-call(s32[1]{0:T(128)} %bitcast.own_ref, s32[16]{0:T(128)S(1)} %get-tuple-element.31.leave_tab, s32[1,12]{1,0:T(1,128)} %leave_hbm.3, s32[4,12]{1,0:T(4,128)} %dest_hbm.3, s32[1,12]{1,0:T(1,128)} %land_hbm.1, ...), custom_call_target="tpu_custom_call" | custom-call | tf_op jit(solution)/shard_map/gather_ssm/pallas_call | solution.py:479
  10.4 1.6 %collective-permute-start.1 = (bf16[4,16,4096]{2,1,0:T(8,128)(2,1)}, bf16[4,16,4096]{2,1,0:T(8,128)(2,1)}, u32[]{:S(2)}, u32[]{:S(2)}) collective-permute-start(bf16[4,16,4096]{2,1,0:T(8,128)(2,1)} %get-tuple-element.34), channel_id=1, source_target_pairs={{0,8},{4,12},{8,0},{12,4},{1,9},{5,13},{9,1},{13,5},{2,10},{6,14},... | collective-permute-start | bytes 1572872 | tf_op jit(solution)/shard_map/ppermute | solution.py:397
  12.0 0.3 collective-permute-start.2
  12.3 0.3 collective-permute-done.5.rest_2_
  12.7 0.0 copy-start.1
  12.7 0.0 copy-start.2
  12.7 0.0 copy-start.3
  12.7 4.3 %project.1 = (f32[96,4096]{1,0:T(8,128)S(1)}, bf16[3,48,4096]{2,1,0:T(8,128)(2,1)}, f32[96,640]{1,0:T(8,128)S(1)}, bf16[96,640]{1,0:T(8,128)(2,1)S(1)}) custom-call(s32[17]{0:T(128)S(1)} %get-tuple-element.33.land_tab, bf16[4,16,4096]{2,1,0:T(8,128)(2,1)S(1)} %collective-permute-done.3._.rest_7_, bf16[48,1024]{1,0:T(8,128)(2,1)S(1)} %collective-permute-done._.rest_0_, ...), custom_call_target="tpu_custom_call" | custom-call | flops 999999995904 | tf_op jit(solution)/shard_map/project/pallas_call | solution.py:500
  17.0 1.6 %collective-permute-start.8 = (bf16[96,640]{1,0:T(8,128)(2,1)S(1)}, bf16[96,640]{1,0:T(8,128)(2,1)S(1)}, u32[]{:S(2)}, u32[]{:S(2)}) collective-permute-start(bf16[96,640]{1,0:T(8,128)(2,1)S(1)} %get-tuple-element.43), channel_id=1, source_target_pairs={{0,1},{1,0},{2,3},{3,2},{4,5},{5,4},{6,7},{7,6},{8,9},{9,8},{10,11... | collective-permute-start | bytes 368648 | tf_op jit(solution)/shard_map/ppermute | solution.py:397
  18.6 2.6 %collective-permute-start.7 = (bf16[96,640]{1,0:T(8,128)(2,1)S(1)}, bf16[96,640]{1,0:T(8,128)(2,1)S(1)}, u32[]{:S(2)}, u32[]{:S(2)}) collective-permute-start(bf16[96,640]{1,0:T(8,128)(2,1)S(1)} %get-tuple-element.43), channel_id=1, source_target_pairs={{0,2},{1,3},{2,0},{3,1},{4,6},{5,7},{6,4},{7,5},{8,10},{9,11},{10,... | collective-permute-start | bytes 368648 | tf_op jit(solution)/shard_map/ppermute | solution.py:397
  21.2 0.3 collective-permute-start.6
  21.5 4.0 %gate.1 = (bf16[48,16,4096]{2,1,0:T(8,128)(2,1)S(1)}, bf16[512,4096]{1,0:T(8,128)(2,1)S(1)}, f32[96,4096]{1,0:T(8,128)S(1)}, f32[96,4096]{1,0:T(8,128)S(1)}, f32[16,4096]{1,0:T(8,128)S(1)}) custom-call(f32[96,4096]{1,0:T(8,128)S(1)} %get-tuple-element.39.conv_out.rest_6_, bf16[96,4096]{1,0:T(8,128)(2,1)S(1)} %bitcast.10, f32[1,4096]{1,0:T(1,128)S(1)} %bitcast.11, ...), custom_call_target="tpu_custom_call" | custom-call | tf_op jit(solution)/shard_map/gate/pallas_call | solution.py:527
  25.5 5.4 %collective-permute-done.7.rest_1_ = bf16[96,640]{1,0:T(8,128)(2,1)S(1)} collective-permute-done((bf16[96,640]{1,0:T(8,128)(2,1)S(1)}, bf16[96,640]{1,0:T(8,128)(2,1)S(1)}, u32[]{:S(2)}, u32[]{:S(2)}) %collective-permute-start.7) | collective-permute-done | bytes 122912 | tf_op jit(solution)/shard_map/ppermute | solution.py:397
  31.0 8.3 %update_staying.1 = (bf16[48,16,4096]{2,1,0:T(8,128)(2,1)}, f32[96,4096]{1,0:T(8,128)S(1)}, f32[96,4096]{1,0:T(8,128)S(1)}, f32[96,16,128]{2,1,0:T(8,128)S(1)}, ...) custom-call(s32[17]{0:T(128)S(1)} %get-tuple-element.33.land_tab, ...), custom_call_target="tpu_custom_call" | custom-call | tf_op jit(solution)/shard_map/update_staying/pallas_call | solution.py:545
  39.3 5.0 %update_arrived.1 = (bf16[2,48,4096]{2,1,0:T(8,128)(2,1)}, bf16[48,16,4096]{2,1,0:T(8,128)(2,1)}) custom-call(s32[17]{0:T(128)S(1)} %get-tuple-element.33.land_tab, bf16[4,16,4096]{2,1,0:T(8,128)(2,1)} %collective-permute-done.1.rest_0_, bf16[4,16,4096]{2,1,0:T(8,128)(2,1)} %collective-permute-done.2.rest_1_, ...), custom_call_target="tpu_custom_call", output_to_operand_aliasing={{1}: (13, {})} | custom-call | tf_op jit(solution)/shard_map/update_arrived/pallas_call | solution.py:576
  (21 shorter events, 0.0 us)
Async XLA Ops:
  0.6 12.0 %slice-start = ((s8[4456448]{0:T(1024)(128)(4,1)}), s8[4194304]{0:T(1024)(128)(4,1)S(1)}, s32[]{:S(2)}) async-start(s8[4456448]{0:T(1024)(128)(4,1)} %bitcast.13), calls=%async_computation | async-start | bytes 8388608
  0.6 12.0 %slice-start.1 = ((s8[4456448]{0:T(1024)(128)(4,1)}), s8[262144]{0:T(1024)(128)(4,1)S(1)}, s32[]{:S(2)}) async-start(s8[4456448]{0:T(1024)(128)(4,1)} %bitcast.13), calls=%async_computation.1 | async-start | bytes 524288
  3.9 8.7 %copy-start = (bf16[48,3,4096]{2,0,1:T(8,128)(2,1)S(1)}, bf16[48,3,4096]{2,0,1:T(8,128)(2,1)}, u32[]{:S(2)}) copy-start(bf16[48,3,4096]{2,0,1:T(8,128)(2,1)} %param.17) | copy-start | bytes 3538948
  3.9 8.7 %copy-start.5 = (bf16[2,48,4096]{2,1,0:T(8,128)(2,1)S(1)}, bf16[2,48,4096]{2,1,0:T(8,128)(2,1)}, u32[]{:S(2)}) copy-start(bf16[2,48,4096]{2,1,0:T(8,128)(2,1)} %rest_4_.1) | copy-start | bytes 2359300
  3.9 8.7 %copy-start.6 = (f32[4,4096]{1,0:T(4,128)S(1)}, f32[4,4096]{1,0:T(4,128)}, u32[]{:S(2)}) copy-start(f32[4,4096]{1,0:T(4,128)} %rest_5_.1) | copy-start | bytes 196612
  3.9 8.7 %copy-start.7 = (f32[4096]{0:T(1024)S(1)}, f32[4096]{0:T(1024)}, u32[]{:S(2)}) copy-start(f32[4096]{0:T(1024)} %param.19) | copy-start | bytes 49156
  3.9 8.7 %collective-permute-start.3 = (bf16[4,16,4096]{2,1,0:T(8,128)(2,1)S(1)}, bf16[4,16,4096]{2,1,0:T(8,128)(2,1)S(1)}, u32[]{:S(2)}, u32[]{:S(2)}) collective-permute-start(bf16[4,16,4096]{2,1,0:T(8,128)(2,1)S(1)} %get-tuple-element.36), channel_id=1, source_target_pairs={{0,4},{4,0},{8,12},{12,8},{1,5},{5,1},{9,13},{13,9},{2,6},{6,2},{1... | collective-permute-start | bytes 1572872 | tf_op jit(solution)/shard_map/ppermute | solution.py:397
  4.4 3.0 %collective-permute-start = (bf16[48,1024]{1,0:T(8,128)(2,1)S(1)}, bf16[48,1024]{1,0:T(8,128)(2,1)S(1)}, u32[]{:S(2)}, u32[]{:S(2)}) collective-permute-start(bf16[48,1024]{1,0:T(8,128)(2,1)S(1)} %get-tuple-element.32), channel_id=1, source_target_pairs={{0,4},{4,0},{8,12},{12,8},{1,5},{5,1},{9,13},{13,9},{2,6},{6,2},{1... | collective-permute-start | bytes 294920 | tf_op jit(solution)/shard_map/ppermute | solution.py:397
  4.5 7.8 %collective-permute-start.4 = (bf16[48,1024]{1,0:T(8,128)(2,1)S(1)}, bf16[48,1024]{1,0:T(8,128)(2,1)S(1)}, u32[]{:S(2)}, u32[]{:S(2)}) collective-permute-start(bf16[48,1024]{1,0:T(8,128)(2,1)S(1)} %get-tuple-element.37), channel_id=1, source_target_pairs={{0,8},{4,12},{8,0},{12,4},{1,9},{5,13},{9,1},{13,5},{2,10},{6,14},... | collective-permute-start | bytes 294920 | tf_op jit(solution)/shard_map/ppermute | solution.py:397
  7.5 5.1 %collective-permute-start.5 = (bf16[48,1024]{1,0:T(8,128)(2,1)S(1)}, bf16[48,1024]{1,0:T(8,128)(2,1)S(1)}, u32[]{:S(2)}, u32[]{:S(2)}) collective-permute-start(bf16[48,1024]{1,0:T(8,128)(2,1)S(1)} %get-tuple-element.38), channel_id=1, source_target_pairs={{0,12},{4,8},{8,4},{12,0},{1,13},{5,9},{9,5},{13,1},{2,14},{6,10},... | collective-permute-start | bytes 294920 | tf_op jit(solution)/shard_map/ppermute | solution.py:397
  10.4 28.9 %collective-permute-start.1 = (bf16[4,16,4096]{2,1,0:T(8,128)(2,1)}, bf16[4,16,4096]{2,1,0:T(8,128)(2,1)}, u32[]{:S(2)}, u32[]{:S(2)}) collective-permute-start(bf16[4,16,4096]{2,1,0:T(8,128)(2,1)} %get-tuple-element.34), channel_id=1, source_target_pairs={{0,8},{4,12},{8,0},{12,4},{1,9},{5,13},{9,1},{13,5},{2,10},{6,14},... | collective-permute-start | bytes 1572872 | tf_op jit(solution)/shard_map/ppermute | solution.py:397
  12.0 27.3 %collective-permute-start.2 = (bf16[4,16,4096]{2,1,0:T(8,128)(2,1)}, bf16[4,16,4096]{2,1,0:T(8,128)(2,1)}, u32[]{:S(2)}, u32[]{:S(2)}) collective-permute-start(bf16[4,16,4096]{2,1,0:T(8,128)(2,1)} %get-tuple-element.35), channel_id=1, source_target_pairs={{0,12},{4,8},{8,4},{12,0},{1,13},{5,9},{9,5},{13,1},{2,14},{6,10},... | collective-permute-start | bytes 1572872 | tf_op jit(solution)/shard_map/ppermute | solution.py:397
  12.7 8.8 %copy-start.1 = (bf16[2,48,4096]{2,1,0:T(8,128)(2,1)S(1)}, bf16[2,48,4096]{2,1,0:T(8,128)(2,1)}, u32[]{:S(2)}) copy-start(bf16[2,48,4096]{2,1,0:T(8,128)(2,1)} %param.15) | copy-start | bytes 2359300
  12.7 8.8 %copy-start.2 = (f32[16,4096]{1,0:T(8,128)S(1)}, f32[16,4096]{1,0:T(8,128)}, u32[]{:S(2)}) copy-start(f32[16,4096]{1,0:T(8,128)} %a_log.1) | copy-start | bytes 786436
  12.7 8.8 %copy-start.3 = (f32[4096]{0:T(1024)S(1)}, f32[4096]{0:T(1024)}, u32[]{:S(2)}) copy-start(f32[4096]{0:T(1024)} %param.24) | copy-start | bytes 49156
  17.0 8.5 %collective-permute-start.8 = (bf16[96,640]{1,0:T(8,128)(2,1)S(1)}, bf16[96,640]{1,0:T(8,128)(2,1)S(1)}, u32[]{:S(2)}, u32[]{:S(2)}) collective-permute-start(bf16[96,640]{1,0:T(8,128)(2,1)S(1)} %get-tuple-element.43), channel_id=1, source_target_pairs={{0,1},{1,0},{2,3},{3,2},{4,5},{5,4},{6,7},{7,6},{8,9},{9,8},{10,11... | collective-permute-start | bytes 368648 | tf_op jit(solution)/shard_map/ppermute | solution.py:397
  18.6 12.4 %collective-permute-start.7 = (bf16[96,640]{1,0:T(8,128)(2,1)S(1)}, bf16[96,640]{1,0:T(8,128)(2,1)S(1)}, u32[]{:S(2)}, u32[]{:S(2)}) collective-permute-start(bf16[96,640]{1,0:T(8,128)(2,1)S(1)} %get-tuple-element.43), channel_id=1, source_target_pairs={{0,2},{1,3},{2,0},{3,1},{4,6},{5,7},{6,4},{7,5},{8,10},{9,11},{10,... | collective-permute-start | bytes 368648 | tf_op jit(solution)/shard_map/ppermute | solution.py:397
  21.2 9.8 %collective-permute-start.6 = (bf16[96,640]{1,0:T(8,128)(2,1)S(1)}, bf16[96,640]{1,0:T(8,128)(2,1)S(1)}, u32[]{:S(2)}, u32[]{:S(2)}) collective-permute-start(bf16[96,640]{1,0:T(8,128)(2,1)S(1)} %get-tuple-element.43), channel_id=1, source_target_pairs={{0,3},{1,2},{2,1},{3,0},{4,7},{5,6},{6,5},{7,4},{8,11},{9,10},{10,... | collective-permute-start | bytes 368648 | tf_op jit(solution)/shard_map/ppermute | solution.py:397
  21.5 9.5 %copy-start.4 = (f32[4096]{0:T(1024)S(1)}, f32[4096]{0:T(1024)}, u32[]{:S(2)}) copy-start(f32[4096]{0:T(1024)} %param.22) | copy-start | bytes 49156

commit v4 on v3

--- a/solution.py
+++ b/solution.py
@@ -14,6 +14,7 @@
 LOG2E = math.log2(math.e)
 MIB = 1 << 20
 PIECE = 512
+PACK = 16
 
 
 def iota(shape, dim):
@@ -173,16 +174,17 @@
             arrived = arrived | (slot_row == slot)
     tap = lax.rem(lax.div(inner, cap), taps)
     chunk = lax.div(inner, taps * cap)
-    grid_row = iota((slots, peers * rows), 0)
+    target = jnp.where(target >= 0, tap * slots + target, -1)
+    grid_row = iota((taps * slots, peers * rows), 0)
     incoming = jnp.concatenate([g[...] for g in got], axis=0)
     total = jnp.zeros((2 * slots, cols), F32)
     for q in range(chunks):
         lanes = slice(q * width, (q + 1) * width)
-        history = []
-        for j in range(taps):
-            pick = grid_row == jnp.where((tap == j) & (chunk == q), target, -1)
-            moved = jnp.dot(jnp.where(pick, 1.0, 0.0).astype(BF16), incoming, preferred_element_type=F32)
-            history.append(jnp.where(arrived, moved, conv[j, :, lanes].astype(F32)))
+        pick = jnp.where(grid_row == jnp.where(chunk == q, target, -1), 1.0, 0.0).astype(BF16)
+        moved = jnp.dot(pick, incoming, preferred_element_type=F32)
+        history = [
+            jnp.where(arrived, moved[j * slots : (j + 1) * slots], conv[j, :, lanes].astype(F32)) for j in range(taps)
+        ]
         newest[:, lanes] = history[taps - 1].astype(BF16)
         window = history + [x_new[t, :, lanes].astype(F32) for t in range(2)]
         halves = []
@@ -200,14 +202,19 @@
             preferred_element_type=F32,
         )
     store[2].start()
-    padded = own_sum.shape[1]
-    rank = padded - LANES
+    rank = own_sum.shape[1] - LANES
     own_sum[:, rank:] = jnp.zeros((2 * slots, LANES), F32)
     own_sum[:, :cols] = total
     tail = own_sum[:, rank:]
-    send_sum[:, :rank] = total[:, :rank].astype(BF16)
+    send_sum[: 2 * slots, :] = total[:, :rank].astype(BF16)
     high = tail.astype(BF16).astype(F32)
-    send_sum[:, rank:] = (high + pltpu.roll(tail - high, cols - rank, 1)).astype(BF16)
+    used = cols - rank
+    pair = high + pltpu.roll(tail - high, used, 1)
+    packed = pair[:slots] + pltpu.roll(pair[slots:], 2 * used, 1)
+    send_sum[2 * slots :, :] = jnp.zeros((PACK, rank), BF16)
+    for at in range(slots // PACK):
+        block = packed[at * PACK : (at + 1) * PACK]
+        send_sum[2 * slots :, at * LANES : (at + 1) * LANES] = block.astype(BF16)
     for copy in store:
         copy.wait()
 
@@ -286,10 +293,13 @@
 
     raw = own_sum[:, :rank]
     tail = own_sum[:, rank:]
+    used = 2 * states
     for g in got:
-        raw += g[:, :rank].astype(F32)
-        piece = g[:, rank:].astype(F32)
-        tail += piece + pltpu.roll(piece, LANES - 2 * states, 1)
+        raw += g[: 2 * slots, :].astype(F32)
+        blocks = [g[2 * slots :, at * LANES : (at + 1) * LANES] for at in range(slots // PACK)]
+        pair = jnp.concatenate(blocks, axis=0).astype(F32)
+        pair += pltpu.roll(pair, LANES - used, 1)
+        tail += jnp.concatenate([pair, pltpu.roll(pair, LANES - 2 * used, 1)], axis=0)
     scale = lax.rsqrt(jnp.mean(raw * raw, axis=1, keepdims=True) + 1e-06)
     normed = (raw * scale).astype(BF16)
     for start in range(0, channels, step):
@@ -503,7 +513,7 @@
                 shape((both, channels), F32),
                 shape((taps, slots, channels), BF16),
                 shape((both, padded), F32),
-                shape((both, padded), BF16),
+                shape((both + PACK, rank), BF16),
             ],
             in_specs=[smem, anywhere] + [vmem] * (peers + 5),
             out_specs=[vmem, hbm, vmem, vmem],
@@ -521,7 +531,7 @@
             proj_t,
         )
 
-    sums_got = [exchange(send_sum, "tp", k, tps) for k in range(tps - 1, 0, -1)]
+    sums_got = [exchange(send_sum, "tp", k, tps) for k in range(1, tps)]
 
     with jax.named_scope("gate"):
         ssm_held, weight_held, gate, skipped, rate = pl.pallas_call(

time: 44.5 us -> 43 us (0.966)
  Pallas kernels: 27.8 us -> 26.7 us
    pallas_call x1, Pallas kernels: 4.31 us -> 3.51 us  [local(): pl.pallas_call(functools.partial(project_kernel, n, cap, chunks), out_sha...]
  transfers between devices with their start and end apart: 9 -> 9, of which waited for: 2 -> 2; matrix products, arithmetic and copies ran while one was open for 0% -> 0% of each run, Pallas kernels for 44% -> 43%
where the time goes in v4:
time: 43 us; the launch traced here: 42.8 us
  Pallas kernels  26.7 us (62%)
  starting transfers between devices  9.89 us (23%)
  waiting for transfers between devices  5.39 us (13%)
  between operations  0.83 us (2%)
    ppermute x9, starting transfers between devices, exchange(): return lax.ppermute(value, axis, [(i, i ^ k) for i in range(n)])  9.89 us
    pallas_call x1, Pallas kernels, local(): pl.pallas_call(functools.partial(stay_kernel, n, tps, cap, stays, step),...  8.1 us
    ppermute x9, waiting for transfers between devices, exchange(): return lax.ppermute(value, axis, [(i, i ^ k) for i in range(n)])  5.39 us
    pallas_call x1, Pallas kernels, local(): pl.pallas_call(functools.partial(arrive_kernel, n, cap, mig, step), out_s...  4.9 us
    pallas_call x1, Pallas kernels, local(): pl.pallas_call(gate_kernel, out_shape=[shape((slots, states, channels), B...  4.03 us
    pallas_call x1, Pallas kernels, local(): pl.pallas_call(functools.partial(project_kernel, n, cap, chunks), out_sha...  3.51 us
    pallas_call x1, Pallas kernels, local(): pl.pallas_call(functools.partial(gather_conv_kernel, n, cap, chunks), out...  3.22 us
    pallas_call x1, Pallas kernels, local(): pl.pallas_call(functools.partial(gather_ssm_kernel, n, cap, far_peers), o...  2.91 us
  transfers between devices with their start and end apart: 9, of which 2 were waited for; matrix products, arithmetic and copies ran while one was open for 0% of the time, Pallas kernels for 43%

profile of v4, /device:TPU:0, one launch (start us, length us, event | category | flops | bytes accessed | tf_op | source)
XLA Modules:
  0.0 42.8 jit_solution(4061264233633950681)
XLA Ops:
  0.6 0.0 slice-start.1
  0.7 3.2 %gather_conv.1 = (bf16[48,1024]{1,0:T(8,128)(2,1)S(1)}, bf16[48,1024]{1,0:T(8,128)(2,1)S(1)}, bf16[48,1024]{1,0:T(8,128)(2,1)S(1)}, bf16[4,16,4096]{2,1,0:T(8,128)(2,1)S(1)}, s32[16]{0:T(128)S(1)}) custom-call(s32[1]{0:T(128)} %bitcast.own_ref, s32[1,12]{1,0:T(1,128)} %leave_hbm.3, s32[4,12]{1,0:T(4,128)} %dest_hbm.3, bf16[3,48,4096]{2,1,0:T(8,128)(2,1)} %bitcast.8, ...), custom_call_target="tpu_custom_call" | custom-call | tf_op jit(solution)/shard_map/gather_conv/pallas_call | solution.py:465
  3.9 0.0 copy-start
  3.9 0.0 copy-start.5
  3.9 0.0 copy-start.6
  3.9 0.0 copy-start.7
  3.9 0.5 %collective-permute-start.3 = (bf16[4,16,4096]{2,1,0:T(8,128)(2,1)S(1)}, bf16[4,16,4096]{2,1,0:T(8,128)(2,1)S(1)}, u32[]{:S(2)}, u32[]{:S(2)}) collective-permute-start(bf16[4,16,4096]{2,1,0:T(8,128)(2,1)S(1)} %get-tuple-element.36), channel_id=1, source_target_pairs={{0,4},{4,0},{8,12},{12,8},{1,5},{5,1},{9,13},{13,9},{2,6},{6,2},{1... | collective-permute-start | bytes 1572872 | tf_op jit(solution)/shard_map/ppermute | solution.py:407
  4.4 0.1 collective-permute-start
  4.5 2.9 %collective-permute-start.4 = (bf16[48,1024]{1,0:T(8,128)(2,1)S(1)}, bf16[48,1024]{1,0:T(8,128)(2,1)S(1)}, u32[]{:S(2)}, u32[]{:S(2)}) collective-permute-start(bf16[48,1024]{1,0:T(8,128)(2,1)S(1)} %get-tuple-element.37), channel_id=1, source_target_pairs={{0,8},{4,12},{8,0},{12,4},{1,9},{5,13},{9,1},{13,5},{2,10},{6,14},... | collective-permute-start | bytes 294920 | tf_op jit(solution)/shard_map/ppermute | solution.py:407
  7.5 0.0 collective-permute-start.5
  7.5 2.9 %gather_ssm.1 = (bf16[4,16,4096]{2,1,0:T(8,128)(2,1)}, bf16[4,16,4096]{2,1,0:T(8,128)(2,1)}, s32[17]{0:T(128)S(1)}, s32[48]{0:T(128)S(1)}) custom-call(s32[1]{0:T(128)} %bitcast.own_ref, s32[16]{0:T(128)S(1)} %get-tuple-element.31.leave_tab, s32[1,12]{1,0:T(1,128)} %leave_hbm.3, s32[4,12]{1,0:T(4,128)} %dest_hbm.3, s32[1,12]{1,0:T(1,128)} %land_hbm.1, ...), custom_call_target="tpu_custom_call" | custom-call | tf_op jit(solution)/shard_map/gather_ssm/pallas_call | solution.py:489
  10.4 1.6 %collective-permute-start.1 = (bf16[4,16,4096]{2,1,0:T(8,128)(2,1)}, bf16[4,16,4096]{2,1,0:T(8,128)(2,1)}, u32[]{:S(2)}, u32[]{:S(2)}) collective-permute-start(bf16[4,16,4096]{2,1,0:T(8,128)(2,1)} %get-tuple-element.34), channel_id=1, source_target_pairs={{0,8},{4,12},{8,0},{12,4},{1,9},{5,13},{9,1},{13,5},{2,10},{6,14},... | collective-permute-start | bytes 1572872 | tf_op jit(solution)/shard_map/ppermute | solution.py:407
  12.0 0.3 collective-permute-start.2
  12.3 0.3 collective-permute-done.5.rest_2_
  12.7 0.0 copy-start.1
  12.7 0.0 copy-start.2
  12.7 0.0 copy-start.3
  12.7 3.5 %project.1 = (f32[96,4096]{1,0:T(8,128)S(1)}, bf16[3,48,4096]{2,1,0:T(8,128)(2,1)}, f32[96,640]{1,0:T(8,128)S(1)}, bf16[112,512]{1,0:T(8,128)(2,1)S(1)}) custom-call(s32[17]{0:T(128)S(1)} %get-tuple-element.33.land_tab, bf16[4,16,4096]{2,1,0:T(8,128)(2,1)S(1)} %collective-permute-done.3._.rest_7_, bf16[48,1024]{1,0:T(8,128)(2,1)S(1)} %collective-permute-done._.rest_0_, ...), custom_call_target="tpu_custom_call" | custom-call | flops 999999995904 | tf_op jit(solution)/shard_map/project/pallas_call | solution.py:510
  16.2 3.6 %collective-permute-start.8 = (bf16[112,512]{1,0:T(8,128)(2,1)S(1)}, bf16[112,512]{1,0:T(8,128)(2,1)S(1)}, u32[]{:S(2)}, u32[]{:S(2)}) collective-permute-start(bf16[112,512]{1,0:T(8,128)(2,1)S(1)} %get-tuple-element.43), channel_id=1, source_target_pairs={{0,3},{1,2},{2,1},{3,0},{4,7},{5,6},{6,5},{7,4},{8,11},{9,10},{10,... | collective-permute-start | bytes 344072 | tf_op jit(solution)/shard_map/ppermute | solution.py:407
  19.8 0.8 %collective-permute-start.6 = (bf16[112,512]{1,0:T(8,128)(2,1)S(1)}, bf16[112,512]{1,0:T(8,128)(2,1)S(1)}, u32[]{:S(2)}, u32[]{:S(2)}) collective-permute-start(bf16[112,512]{1,0:T(8,128)(2,1)S(1)} %get-tuple-element.43), channel_id=1, source_target_pairs={{0,1},{1,0},{2,3},{3,2},{4,5},{5,4},{6,7},{7,6},{8,9},{9,8},{10,11... | collective-permute-start | bytes 344072 | tf_op jit(solution)/shard_map/ppermute | solution.py:407
  20.7 4.0 %gate.1 = (bf16[48,16,4096]{2,1,0:T(8,128)(2,1)S(1)}, bf16[512,4096]{1,0:T(8,128)(2,1)S(1)}, f32[96,4096]{1,0:T(8,128)S(1)}, f32[96,4096]{1,0:T(8,128)S(1)}, f32[16,4096]{1,0:T(8,128)S(1)}) custom-call(f32[96,4096]{1,0:T(8,128)S(1)} %get-tuple-element.39.conv_out.rest_6_, bf16[96,4096]{1,0:T(8,128)(2,1)S(1)} %bitcast.10, f32[1,4096]{1,0:T(1,128)S(1)} %bitcast.11, ...), custom_call_target="tpu_custom_call" | custom-call | tf_op jit(solution)/shard_map/gate/pallas_call | solution.py:537
  24.7 5.0 %collective-permute-done.7.rest_1_ = bf16[112,512]{1,0:T(8,128)(2,1)S(1)} collective-permute-done((bf16[112,512]{1,0:T(8,128)(2,1)S(1)}, bf16[112,512]{1,0:T(8,128)(2,1)S(1)}, u32[]{:S(2)}, u32[]{:S(2)}) %collective-permute-start.7) | collective-permute-done | bytes 114720 | tf_op jit(solution)/shard_map/ppermute | solution.py:407
  29.8 8.1 %update_staying.1 = (bf16[48,16,4096]{2,1,0:T(8,128)(2,1)}, f32[96,4096]{1,0:T(8,128)S(1)}, f32[96,4096]{1,0:T(8,128)S(1)}, f32[96,16,128]{2,1,0:T(8,128)S(1)}, ...) custom-call(s32[17]{0:T(128)S(1)} %get-tuple-element.33.land_tab, ...), custom_call_target="tpu_custom_call" | custom-call | tf_op jit(solution)/shard_map/update_staying/pallas_call | solution.py:555
  37.9 4.9 %update_arrived.1 = (bf16[2,48,4096]{2,1,0:T(8,128)(2,1)}, bf16[48,16,4096]{2,1,0:T(8,128)(2,1)}) custom-call(s32[17]{0:T(128)S(1)} %get-tuple-element.33.land_tab, bf16[4,16,4096]{2,1,0:T(8,128)(2,1)} %collective-permute-done.1.rest_0_, bf16[4,16,4096]{2,1,0:T(8,128)(2,1)} %collective-permute-done.2.rest_1_, ...), custom_call_target="tpu_custom_call", output_to_operand_aliasing={{1}: (13, {})} | custom-call | tf_op jit(solution)/shard_map/update_arrived/pallas_call | solution.py:586
  (21 shorter events, 0.0 us)
Async XLA Ops:
  0.6 12.0 %slice-start = ((s8[4456448]{0:T(1024)(128)(4,1)}), s8[4194304]{0:T(1024)(128)(4,1)S(1)}, s32[]{:S(2)}) async-start(s8[4456448]{0:T(1024)(128)(4,1)} %bitcast.13), calls=%async_computation | async-start | bytes 8388608
  0.6 12.0 %slice-start.1 = ((s8[4456448]{0:T(1024)(128)(4,1)}), s8[262144]{0:T(1024)(128)(4,1)S(1)}, s32[]{:S(2)}) async-start(s8[4456448]{0:T(1024)(128)(4,1)} %bitcast.13), calls=%async_computation.1 | async-start | bytes 524288
  3.9 8.7 %copy-start = (bf16[48,3,4096]{2,0,1:T(8,128)(2,1)S(1)}, bf16[48,3,4096]{2,0,1:T(8,128)(2,1)}, u32[]{:S(2)}) copy-start(bf16[48,3,4096]{2,0,1:T(8,128)(2,1)} %param.17) | copy-start | bytes 3538948
  3.9 8.7 %copy-start.5 = (bf16[2,48,4096]{2,1,0:T(8,128)(2,1)S(1)}, bf16[2,48,4096]{2,1,0:T(8,128)(2,1)}, u32[]{:S(2)}) copy-start(bf16[2,48,4096]{2,1,0:T(8,128)(2,1)} %rest_4_.1) | copy-start | bytes 2359300
  3.9 8.7 %copy-start.6 = (f32[4,4096]{1,0:T(4,128)S(1)}, f32[4,4096]{1,0:T(4,128)}, u32[]{:S(2)}) copy-start(f32[4,4096]{1,0:T(4,128)} %rest_5_.1) | copy-start | bytes 196612
  3.9 8.7 %copy-start.7 = (f32[4096]{0:T(1024)S(1)}, f32[4096]{0:T(1024)}, u32[]{:S(2)}) copy-start(f32[4096]{0:T(1024)} %param.19) | copy-start | bytes 49156
  3.9 8.7 %collective-permute-start.3 = (bf16[4,16,4096]{2,1,0:T(8,128)(2,1)S(1)}, bf16[4,16,4096]{2,1,0:T(8,128)(2,1)S(1)}, u32[]{:S(2)}, u32[]{:S(2)}) collective-permute-start(bf16[4,16,4096]{2,1,0:T(8,128)(2,1)S(1)} %get-tuple-element.36), channel_id=1, source_target_pairs={{0,4},{4,0},{8,12},{12,8},{1,5},{5,1},{9,13},{13,9},{2,6},{6,2},{1... | collective-permute-start | bytes 1572872 | tf_op jit(solution)/shard_map/ppermute | solution.py:407
  4.4 3.0 %collective-permute-start = (bf16[48,1024]{1,0:T(8,128)(2,1)S(1)}, bf16[48,1024]{1,0:T(8,128)(2,1)S(1)}, u32[]{:S(2)}, u32[]{:S(2)}) collective-permute-start(bf16[48,1024]{1,0:T(8,128)(2,1)S(1)} %get-tuple-element.32), channel_id=1, source_target_pairs={{0,4},{4,0},{8,12},{12,8},{1,5},{5,1},{9,13},{13,9},{2,6},{6,2},{1... | collective-permute-start | bytes 294920 | tf_op jit(solution)/shard_map/ppermute | solution.py:407
  4.5 7.8 %collective-permute-start.4 = (bf16[48,1024]{1,0:T(8,128)(2,1)S(1)}, bf16[48,1024]{1,0:T(8,128)(2,1)S(1)}, u32[]{:S(2)}, u32[]{:S(2)}) collective-permute-start(bf16[48,1024]{1,0:T(8,128)(2,1)S(1)} %get-tuple-element.37), channel_id=1, source_target_pairs={{0,8},{4,12},{8,0},{12,4},{1,9},{5,13},{9,1},{13,5},{2,10},{6,14},... | collective-permute-start | bytes 294920 | tf_op jit(solution)/shard_map/ppermute | solution.py:407
  7.5 5.1 %collective-permute-start.5 = (bf16[48,1024]{1,0:T(8,128)(2,1)S(1)}, bf16[48,1024]{1,0:T(8,128)(2,1)S(1)}, u32[]{:S(2)}, u32[]{:S(2)}) collective-permute-start(bf16[48,1024]{1,0:T(8,128)(2,1)S(1)} %get-tuple-element.38), channel_id=1, source_target_pairs={{0,12},{4,8},{8,4},{12,0},{1,13},{5,9},{9,5},{13,1},{2,14},{6,10},... | collective-permute-start | bytes 294920 | tf_op jit(solution)/shard_map/ppermute | solution.py:407
  10.4 27.5 %collective-permute-start.1 = (bf16[4,16,4096]{2,1,0:T(8,128)(2,1)}, bf16[4,16,4096]{2,1,0:T(8,128)(2,1)}, u32[]{:S(2)}, u32[]{:S(2)}) collective-permute-start(bf16[4,16,4096]{2,1,0:T(8,128)(2,1)} %get-tuple-element.34), channel_id=1, source_target_pairs={{0,8},{4,12},{8,0},{12,4},{1,9},{5,13},{9,1},{13,5},{2,10},{6,14},... | collective-permute-start | bytes 1572872 | tf_op jit(solution)/shard_map/ppermute | solution.py:407
  12.0 25.9 %collective-permute-start.2 = (bf16[4,16,4096]{2,1,0:T(8,128)(2,1)}, bf16[4,16,4096]{2,1,0:T(8,128)(2,1)}, u32[]{:S(2)}, u32[]{:S(2)}) collective-permute-start(bf16[4,16,4096]{2,1,0:T(8,128)(2,1)} %get-tuple-element.35), channel_id=1, source_target_pairs={{0,12},{4,8},{8,4},{12,0},{1,13},{5,9},{9,5},{13,1},{2,14},{6,10},... | collective-permute-start | bytes 1572872 | tf_op jit(solution)/shard_map/ppermute | solution.py:407
  12.7 8.0 %copy-start.1 = (bf16[2,48,4096]{2,1,0:T(8,128)(2,1)S(1)}, bf16[2,48,4096]{2,1,0:T(8,128)(2,1)}, u32[]{:S(2)}) copy-start(bf16[2,48,4096]{2,1,0:T(8,128)(2,1)} %param.15) | copy-start | bytes 2359300
  12.7 8.0 %copy-start.2 = (f32[16,4096]{1,0:T(8,128)S(1)}, f32[16,4096]{1,0:T(8,128)}, u32[]{:S(2)}) copy-start(f32[16,4096]{1,0:T(8,128)} %a_log.1) | copy-start | bytes 786436
  12.7 8.0 %copy-start.3 = (f32[4096]{0:T(1024)S(1)}, f32[4096]{0:T(1024)}, u32[]{:S(2)}) copy-start(f32[4096]{0:T(1024)} %param.24) | copy-start | bytes 49156
  16.2 8.5 %collective-permute-start.8 = (bf16[112,512]{1,0:T(8,128)(2,1)S(1)}, bf16[112,512]{1,0:T(8,128)(2,1)S(1)}, u32[]{:S(2)}, u32[]{:S(2)}) collective-permute-start(bf16[112,512]{1,0:T(8,128)(2,1)S(1)} %get-tuple-element.43), channel_id=1, source_target_pairs={{0,3},{1,2},{2,1},{3,0},{4,7},{5,6},{6,5},{7,4},{8,11},{9,10},{10,... | collective-permute-start | bytes 344072 | tf_op jit(solution)/shard_map/ppermute | solution.py:407
  19.8 10.0 %collective-permute-start.7 = (bf16[112,512]{1,0:T(8,128)(2,1)S(1)}, bf16[112,512]{1,0:T(8,128)(2,1)S(1)}, u32[]{:S(2)}, u32[]{:S(2)}) collective-permute-start(bf16[112,512]{1,0:T(8,128)(2,1)S(1)} %get-tuple-element.43), channel_id=1, source_target_pairs={{0,2},{1,3},{2,0},{3,1},{4,6},{5,7},{6,4},{7,5},{8,10},{9,11},{10,... | collective-permute-start | bytes 344072 | tf_op jit(solution)/shard_map/ppermute | solution.py:407
  19.8 10.0 %collective-permute-start.6 = (bf16[112,512]{1,0:T(8,128)(2,1)S(1)}, bf16[112,512]{1,0:T(8,128)(2,1)S(1)}, u32[]{:S(2)}, u32[]{:S(2)}) collective-permute-start(bf16[112,512]{1,0:T(8,128)(2,1)S(1)} %get-tuple-element.43), channel_id=1, source_target_pairs={{0,1},{1,0},{2,3},{3,2},{4,5},{5,4},{6,7},{7,6},{8,9},{9,8},{10,11... | collective-permute-start | bytes 344072 | tf_op jit(solution)/shard_map/ppermute | solution.py:407
  20.7 9.1 %copy-start.4 = (f32[4096]{0:T(1024)S(1)}, f32[4096]{0:T(1024)}, u32[]{:S(2)}) copy-start(f32[4096]{0:T(1024)} %param.22) | copy-start | bytes 49156
